TPU v7x, 32 devices: a whole 2x2x4 slice. The times are simulated.
32 devices in a mesh: stream: 8 (over z, core), girth: 4 (over y, x).
Axes of the slice: x: 2, y: 2, z: 4, core: 2. Of those that a mesh axis runs over, the one named last changes fastest.
Arguments:
- state: float32 [16, 7, 32, 128], P('stream', None, 'girth'), may hold values from -1.8 to 1.8
- propeller: float32 [7, 8192], P(None, ('stream', 'girth')), may hold values from -6 to 6
- donor_index: int32 [32, 32], P(('stream', 'girth')), may hold values from -1 to 255, as said below
- fringe_index: int32 [32, 32], P(('stream', 'girth')), may hold values from -1 to 2047, as said below
- donor_weight: float32 [32, 32], P(('stream', 'girth')), may hold values from 0.25 to 1
- disk_mask: int32 [16, 32, 128], P('stream', 'girth'), may hold values 0 or 1
- thrust: float32 [7], replicated, may hold values from -1.8 to 1.8
- face: float32 [16, 6, 32, 128], P('stream', None, 'girth'), may hold values from 0.2 to 1
- coupling: float32 [6, 7, 7], replicated, may hold values from -0.875 to 0.875
- diag_inverse: bfloat16 [16, 7, 7, 32, 128], P('stream', None, None, 'girth'), may hold values from -0.15039062 to 1
- lower_jacobian: float32 [7, 7], replicated, may hold values from -0.06 to 1.06
- upper_jacobian: float32 [7, 7], replicated, may hold values from -0.06 to 1.06
Outputs:
- new_state: float32 [16, 7, 32, 128], P('stream', None, 'girth')
- residual: float32 [16, 7, 32, 128], P('stream', None, 'girth')
Inputs may be any that keep to these rules, and one draw needn't show every extreme that they name: `donor_index`: live slots of one device and peer come first; every device of one streamwise index fills all 8 slots toward one common peer. `fringe_index`: equal to -1 exactly where donor_index is -1.
All inputs are finite; a program needn't handle non-finite values. No bound on the sum of `disk_mask` on one device may be relied on, other than what follows from the above.
Results may differ from a plain program's by a relative error of at most 0.0003.
Values sent between devices are 32-bit elements; how exact they have to be, the bound alone decides.
A program may use at most 64 MiB of HBM per device.

v0:
```python
import jax
import jax.numpy as jnp
from jax import lax
from jax.sharding import PartitionSpec as P

PRECISE = lax.Precision.HIGHEST


def extended(block, sides, width, periodic):
    for axis, dim in sides:
        count = lax.axis_size(axis)
        forward = [(i, i + 1) for i in range(count - 1)]
        if periodic:
            forward.append((count - 1, 0))
        backward = [(target, source) for source, target in forward]
        low = lax.ppermute(
            lax.slice_in_dim(block, block.shape[dim] - width, None, axis=dim), axis, forward
        )
        high = lax.ppermute(lax.slice_in_dim(block, 0, width, axis=dim), axis, backward)
        block = jnp.concatenate([low, block, high], axis=dim)
    return block


def prefix(shard, axis, combine, identity, reverse):
    count, place = (lax.axis_size(axis), lax.axis_index(axis))
    everything = jax.tree.map(lambda part: lax.all_gather(part, axis), shard)
    start = jax.tree.map(
        lambda part, zero: jnp.broadcast_to(jnp.asarray(zero, part.dtype), part.shape),
        shard,
        identity,
    )

    def turn(k, before):
        at = count - 1 - k if reverse else k
        reached = at > place if reverse else at < place
        new = combine(before, jax.tree.map(lambda part: part[at], everything))
        return jax.tree.map(lambda a, b: jnp.where(reached, a, b), new, before)

    return lax.fori_loop(0, count, turn, start)


def residual_from(current, stream_pad, beside_all, face, coupling, disk_mask, thrust):
    normal_pad = jnp.pad(current, ((0, 0), (0, 0), (0, 0), (1, 1)))
    beside = [
        stream_pad[:-2],
        stream_pad[2:],
        beside_all[:, :, :-2],
        beside_all[:, :, 2:],
        normal_pad[..., :-2],
        normal_pad[..., 2:],
    ]
    residual = disk_mask.astype(jnp.float32)[:, None] * thrust[None, :, None, None]
    for direction in range(6):
        residual = residual + face[:, direction : direction + 1] * jnp.einsum(
            "ij,ajbc->aibc", coupling[direction], beside[direction] - current, precision=PRECISE
        )
    return residual


def forward_step(matrix):

    def advance(previous, inputs):
        inverse, source = inputs
        inverse = inverse.astype(jnp.float32)
        result = jnp.einsum(
            "ijc,jc->ic",
            inverse,
            source + jnp.dot(matrix, previous, precision=PRECISE),
            precision=PRECISE,
        )
        return (result, result)

    return advance


def backward_step(matrix):

    def advance(following, inputs):
        inverse, star = inputs
        inverse = inverse.astype(jnp.float32)
        result = star + jnp.einsum(
            "ijc,jc->ic", inverse, jnp.dot(matrix, following, precision=PRECISE), precision=PRECISE
        )
        return (result, result)

    return advance


def unit_maps(columns):
    return jnp.broadcast_to(jnp.eye(7, dtype=jnp.float32)[:, :, None], (7, 7, columns))


def forward_maps(inverse, source, matrix):

    def advance(carried, inputs):
        compound, start_offset = carried
        block, term = inputs
        block = block.astype(jnp.float32)
        factor = jnp.einsum("ijc,jk->ikc", block, matrix, precision=PRECISE)
        compound = jnp.einsum("ijc,jkc->ikc", factor, compound, precision=PRECISE)
        start_offset = jnp.einsum(
            "ijc,jc->ic",
            block,
            term + jnp.dot(matrix, start_offset, precision=PRECISE),
            precision=PRECISE,
        )
        return ((compound, start_offset), None)

    columns = source.shape[2]
    start = (unit_maps(columns), jnp.zeros((7, columns), jnp.float32))
    result, _ = lax.scan(advance, start, (inverse, source))
    return result


def backward_maps(inverse, stars, matrix):

    def advance(carried, inputs):
        compound, start_offset = carried
        block, star = inputs
        block = block.astype(jnp.float32)
        factor = jnp.einsum("ijc,jk->ikc", block, matrix, precision=PRECISE)
        compound = jnp.einsum("ijc,jkc->ikc", factor, compound, precision=PRECISE)
        start_offset = star + jnp.einsum(
            "ijc,jc->ic", block, jnp.dot(matrix, start_offset, precision=PRECISE), precision=PRECISE
        )
        return ((compound, start_offset), None)

    columns = stars.shape[2]
    start = (unit_maps(columns), jnp.zeros((7, columns), jnp.float32))
    result, _ = lax.scan(advance, start, (inverse, stars), reverse=True)
    return result


def compose(earlier, later_map):
    return (
        jnp.einsum("ijc,jkc->ikc", later_map[0], earlier[0], precision=PRECISE),
        jnp.einsum("ijc,jc->ic", later_map[0], earlier[1], precision=PRECISE) + later_map[1],
    )


def identity_of(maps):
    return (unit_maps(maps[1].shape[1]), jnp.zeros_like(maps[1]))


def sweep_pair(inverse, source, lower, upper, forward_chain, backward_chain):
    maps = forward_maps(inverse, source, lower)
    entry = forward_chain(maps)[1]
    _, stars = lax.scan(forward_step(lower), entry, (inverse, source))
    later_maps = backward_maps(inverse, stars, upper)
    exit_value = backward_chain(later_maps)[1]
    _, updates = lax.scan(backward_step(upper), exit_value, (inverse, stars), reverse=True)
    return updates


def per_device(
    state,
    propeller,
    donor_index,
    fringe_index,
    donor_weight,
    disk_mask,
    thrust,
    face,
    coupling,
    diag_inverse,
    lower_jacobian,
    upper_jacobian,
):
    row_count, var_count, girth_cells, normal_cells = state.shape
    columns = girth_cells * normal_cells
    cell_count = row_count * columns
    is_live = donor_index >= 0
    outgoing = jnp.take(propeller, jnp.maximum(donor_index[0], 0), axis=1) * jnp.where(
        is_live, donor_weight, 0.0
    )
    target = jnp.where(is_live, fringe_index, -1)
    incoming, landing = (
        lax.all_to_all(outgoing, "girth", split_axis=1, concat_axis=1, tiled=True),
        lax.all_to_all(target, "girth", split_axis=1, concat_axis=1, tiled=True),
    )
    flat_index = jnp.where(landing[0] >= 0, landing[0], cell_count)
    accumulated = (
        jnp.zeros((cell_count, var_count), jnp.float32).at[flat_index].add(incoming.T, mode="drop")
    )
    hit_count = jnp.zeros((cell_count,), jnp.int32).at[flat_index].add(1, mode="drop")
    fringe = (hit_count > 0).reshape(row_count, 1, girth_cells, normal_cells)
    donated = accumulated.reshape(row_count, girth_cells, normal_cells, var_count).transpose(
        0, 3, 1, 2
    )
    current = jnp.where(fringe, donated, state)
    stream_pad = extended(current, (("stream", 0),), 1, False)
    beside_all = extended(current, (("girth", 2),), 1, True)
    residual = residual_from(current, stream_pad, beside_all, face, coupling, disk_mask, thrust)
    source = jnp.where(fringe, 0.0, -residual).reshape(row_count, var_count, columns)
    inverse = diag_inverse.reshape(row_count, var_count, var_count, columns)

    def forward_chain(maps):
        return prefix(maps, "stream", compose, identity_of(maps), False)

    def backward_chain(maps):
        return prefix(maps, "stream", compose, identity_of(maps), True)

    updates = sweep_pair(
        inverse, source, lower_jacobian, upper_jacobian, forward_chain, backward_chain
    )
    new_state = current + updates.reshape(row_count, var_count, girth_cells, normal_cells)
    return (new_state, residual)


def solution(mesh):
    placed = (
        P("stream", None, "girth", None),
        P(None, ("stream", "girth")),
        P(("stream", "girth"), None),
        P(("stream", "girth"), None),
        P(("stream", "girth"), None),
        P("stream", "girth", None),
        P(),
        P("stream", None, "girth", None),
        P(),
        P("stream", None, None, "girth", None),
        P(),
        P(),
    )
    return jax.shard_map(
        per_device,
        mesh=mesh,
        in_specs=placed,
        out_specs=(P("stream", None, "girth", None), P("stream", None, "girth", None)),
        check_vma=False,
    )
```

profile of v0, /device:TPU:0, one launch (start us, length us, event | category | flops | bytes accessed | tf_op | source)
XLA Modules:
  0.0 199.9 jit_solution(7371077517450107120)
XLA Ops:
  8.5 5.2 %all-to-all-start = ((s32[1,4,8]{2,0,1:T(1,128)}), s32[1,4,8]{2,0,1:T(1,128)S(1)}, u32[]{:S(2)}, u32[]{:S(2)}) async-start(s32[1,4,8]{2,0,1:T(1,128)} %bitcast.29), calls=%async_computation | async-start | bytes 4096 | tf_op jit(solution)/shard_map/all_to_all | solution.py:179
  14.4 0.8 copy.38
  16.1 0.8 slice_bitcast_fusion
  16.9 0.7 convert_element_type.20
  17.6 1.2 reshape.153
  20.0 0.8 copy.44
  20.8 4.2 %all-to-all-start.1 = ((f32[7,4,8]{0,2,1:T(8,128)}), f32[7,4,8]{0,2,1:T(8,128)S(1)}, u32[]{:S(2)}, u32[]{:S(2)}) async-start(f32[7,4,8]{0,2,1:T(8,128)} %fusion.49), calls=%async_computation.1 | async-start | bytes 32768 | tf_op jit(solution)/shard_map/all_to_all | solution.py:178
  26.2 0.7 scatter_custom_fusion
  27.0 2.7 %all-to-all-done.1 = f32[7,4,8]{0,2,1:T(8,128)S(1)} async-done(((f32[7,4,8]{0,2,1:T(8,128)}), f32[7,4,8]{0,2,1:T(8,128)S(1)}, u32[]{:S(2)}, u32[]{:S(2)}) %all-to-all-start.1) | async-done | bytes 928 | tf_op jit(solution)/shard_map/all_to_all | solution.py:178
  29.7 1.0 scatter_custom_fusion.1
  31.0 0.9 bitcast_select_fusion
  31.8 1.3 collective-permute-start
  33.2 1.3 collective-permute-start.1
  35.1 2.3 %collective-permute-start.3 = (f32[2,7,1,128]{3,1,2,0:T(8,128)S(1)}, f32[2,7,1,128]{3,1,2,0:T(8,128)S(1)}, u32[]{:S(2)}, u32[]{:S(2)}) collective-permute-start(f32[2,7,1,128]{3,1,2,0:T(8,128)S(1)} %get-tuple-element.727), channel_id=1, source_target_pairs={{1,0},{2,1},{3,2},{0,3},{5,4},{6,5},{7,6},{4,7},{9,8},{10,9},{11,1... | collective-permute-start | bytes 21512 | tf_op jit(solution)/shard_map/ppermute | solution.py:19
  37.4 0.9 fusion.29
  38.3 0.9 fusion.27
  39.2 0.9 fusion.25
  40.1 0.9 fusion.23
  41.0 1.0 fusion.21
  42.0 1.0 fusion.19
  43.0 2.2 %broadcast_in_dim.86.clone = f32[7,7,1024]{1,0,2:T(8,128)} broadcast(f32[7,7]{1,0:T(8,128)S(1)} %fusion.64), dimensions={0,1} | broadcast | bytes 200900 | tf_op jit(solution)/shard_map/broadcast_in_dim | solution.py:90
  45.2 31.2 %while.87 = (s32[]{:T(128)}, f32[7,7,1024]{1,0,2:T(8,128)}, f32[7,1024]{0,1:T(8,128)S(1)}, bf16[2,7,7,1024]{3,2,1,0:T(8,128)(2,1)S(1)}, f32[7,7]{0,1:T(8,128)S(1)}, /*index=5*/f32[2,7,1024]{2,1,0:T(8,128)S(1)}, s32[]{:T(128)}) while((s32[]{:T(128)}, f32[7,7,1024]{1,0,2:T(8,128)}, f32[7,1024]{0,1:T(8,128)S(1)}, ...), condition=%wide.region_3.4_spmd, body=%wide.region_2.3_spmd.sunk | while | flops 9182210 | bytes 2828601 | solution.py:111
  46.3 2.7 %copy.110 = f32[7,7,1024]{0,1,2:T(8,128)} copy(f32[7,7,1024]{2,0,1:T(8,128)S(1)} %convolution_bitcast_fusion.12) | data formatting | bytes 401408 | tf_op jit(solution)/shard_map/while/body/eval_jaxpr/ijc,jk->ikc/dot_general | solution.py:99
  49.1 2.3 %copy.169 = f32[7,7,1024]{1,0,2:T(8,128)S(1)} copy(f32[7,7,1024]{1,0,2:T(8,128)} %get-tuple-element.961) | data formatting | bytes 401408 | tf_op jit(solution)/shard_map/while
  51.4 1.1 copy-done
  52.5 8.3 %convolution_bitcast_fusion.13 = f32[7,7,1024]{1,0,2:T(8,128)} fusion(f32[7,7,1024]{0,1,2:T(8,128)S(1)} %copy-done, f32[7,7,1024]{1,0,2:T(8,128)S(1)} %copy.169), kind=kOutput, calls=%fused_computation.3.clone.1 | convolution fusion | flops 4214784 | bytes 602112 | tf_op jit(solution)/shard_map/while/body/eval_jaxpr/ijc,jkc->ikc/dot_general | solution.py:100
  61.9 2.7 %copy.110 = f32[7,7,1024]{0,1,2:T(8,128)} copy(f32[7,7,1024]{2,0,1:T(8,128)S(1)} %convolution_bitcast_fusion.12) | data formatting | bytes 401408 | tf_op jit(solution)/shard_map/while/body/eval_jaxpr/ijc,jk->ikc/dot_general | solution.py:99
  64.6 2.3 %copy.169 = f32[7,7,1024]{1,0,2:T(8,128)S(1)} copy(f32[7,7,1024]{1,0,2:T(8,128)} %get-tuple-element.961) | data formatting | bytes 401408 | tf_op jit(solution)/shard_map/while
  67.0 1.1 copy-done
  68.1 8.3 %convolution_bitcast_fusion.13 = f32[7,7,1024]{1,0,2:T(8,128)} fusion(f32[7,7,1024]{0,1,2:T(8,128)S(1)} %copy-done, f32[7,7,1024]{1,0,2:T(8,128)S(1)} %copy.169), kind=kOutput, calls=%fused_computation.3.clone.1 | convolution fusion | flops 4214784 | bytes 602112 | tf_op jit(solution)/shard_map/while/body/eval_jaxpr/ijc,jkc->ikc/dot_general | solution.py:100
  76.4 3.4 %copy.45 = f32[7,7,1024]{2,1,0:T(8,128)} copy(f32[7,7,1024]{1,0,2:T(8,128)} %get-tuple-element.538) | data formatting | bytes 401408 | tf_op jit(solution)/shard_map/while | solution.py:111
  80.2 17.7 %all-gather.4 = f32[8,7,1024]{2,1,0:T(8,128)S(1)} all-gather(f32[1,7,1024]{2,1,0:T(8,128)S(1)} %bitcast.304), channel_id=3, replica_groups=mesh['stream'=8,'girth'=4] {'stream'}, dimensions={0}, use_global_device_ids=true | all-gather | bytes 258048 | tf_op jit(solution)/shard_map/all_gather | solution.py:26
  98.0 13.6 %all-gather.9.cloned.1.call-done = f32[56,7,1024]{2,1,0:T(8,128)} async-done(((f32[7,7,1024]{2,1,0:T(8,128)}), f32[56,7,1024]{2,1,0:T(8,128)}) %all-gather.9.cloned.1.call-update) | async-done | bytes 1605648 | tf_op jit(solution)/shard_map/all_gather | solution.py:26
  111.5 8.6 %while.90 = (s32[]{:T(128)}, f32[7,1024]{1,0:T(8,128)S(1)}, s32[]{:T(128)}, f32[8,7,7,1024]{3,2,1,0:T(8,128)}, f32[8,7,1024]{2,1,0:T(8,128)S(1)}, /*index=5*/s32[]{:T(128)}, s32[]{:T(128)}) while((s32[]{:T(128)}, f32[7,1024]{1,0:T(8,128)S(1)}, s32[]{:T(128)}, f32[8,7,7,1024]{3,2,1,0:T(8,128)}, f32[8,7,1024]{2,1,0:T(8,128)S(1)}, ...), condition=%wide.region_5.6_spmd.clone, body=%wide.region_4.5_spmd.clone.sunk | while | flops 121860 | bytes 430186 | solution.py:39
  111.5 1.0 fusion.121
  112.6 1.0 fusion.121
  113.7 1.0 fusion.121
  114.8 1.0 fusion.121
  115.8 1.0 fusion.121
  116.9 1.0 fusion.121
  118.0 1.0 fusion.121
  119.1 1.0 fusion.121
  120.8 2.2 %broadcast_in_dim.86 = f32[7,7,1024]{1,0,2:T(8,128)} broadcast(f32[7,7]{1,0:T(8,128)S(1)} %fusion.64), dimensions={0,1} | broadcast | bytes 200900 | tf_op jit(solution)/shard_map/broadcast_in_dim | solution.py:90
  123.0 30.1 %while.91 = (s32[]{:T(128)}, f32[7,7,1024]{1,0,2:T(8,128)}, f32[7,1024]{1,0:T(8,128)S(1)}, bf16[2,7,7,1024]{3,2,1,0:T(8,128)(2,1)S(1)}, f32[7,7]{0,1:T(8,128)S(1...) while((s32[]{:T(128)}, f32[7,7,1024]{1,0,2:T(8,128)}, f32[7,1024]{1,0:T(8,128)S(1)}, ...), condition=%wide.region_9.10_spmd.clone, body=%wide.region_8.9_spmd.clone.sunk | while | flops 9189380 | bytes 2828631 | solution.py:130
  123.6 2.7 %copy.112 = f32[7,7,1024]{0,1,2:T(8,128)} copy(f32[7,7,1024]{2,0,1:T(8,128)S(1)} %convolution_bitcast_fusion.15) | data formatting | bytes 401408 | tf_op jit(solution)/shard_map/while/body/eval_jaxpr/ijc,jk->ikc/dot_general | solution.py:121
  126.2 2.3 %copy.170 = f32[7,7,1024]{1,0,2:T(8,128)S(1)} copy(f32[7,7,1024]{1,0,2:T(8,128)} %get-tuple-element.1025) | data formatting | bytes 401408 | tf_op jit(solution)/shard_map/while
  128.6 1.1 copy-done.1
  129.7 8.4 %convolution_bitcast_fusion.16 = f32[7,7,1024]{1,0,2:T(8,128)} fusion(f32[7,7,1024]{0,1,2:T(8,128)S(1)} %copy-done.1, f32[7,7,1024]{1,0,2:T(8,128)S(1)} %copy.170), kind=kOutput, calls=%fused_computation.25.clone.1 | convolution fusion | flops 4214784 | bytes 602112 | tf_op jit(solution)/shard_map/while/body/eval_jaxpr/ijc,jkc->ikc/dot_general | solution.py:122
  138.6 2.7 %copy.112 = f32[7,7,1024]{0,1,2:T(8,128)} copy(f32[7,7,1024]{2,0,1:T(8,128)S(1)} %convolution_bitcast_fusion.15) | data formatting | bytes 401408 | tf_op jit(solution)/shard_map/while/body/eval_jaxpr/ijc,jk->ikc/dot_general | solution.py:121
  141.3 2.3 %copy.170 = f32[7,7,1024]{1,0,2:T(8,128)S(1)} copy(f32[7,7,1024]{1,0,2:T(8,128)} %get-tuple-element.1025) | data formatting | bytes 401408 | tf_op jit(solution)/shard_map/while
  143.6 1.1 copy-done.1
  144.7 8.4 %convolution_bitcast_fusion.16 = f32[7,7,1024]{1,0,2:T(8,128)} fusion(f32[7,7,1024]{0,1,2:T(8,128)S(1)} %copy-done.1, f32[7,7,1024]{1,0,2:T(8,128)S(1)} %copy.170), kind=kOutput, calls=%fused_computation.25.clone.1 | convolution fusion | flops 4214784 | bytes 602112 | tf_op jit(solution)/shard_map/while/body/eval_jaxpr/ijc,jkc->ikc/dot_general | solution.py:122
  153.1 3.4 %copy.50 = f32[7,7,1024]{2,1,0:T(8,128)} copy(f32[7,7,1024]{1,0,2:T(8,128)} %get-tuple-element.542) | data formatting | bytes 401408 | tf_op jit(solution)/shard_map/while | solution.py:130
  157.2 14.9 %all-gather.5 = f32[8,7,1024]{2,1,0:T(8,128)S(1)} all-gather(f32[1,7,1024]{2,1,0:T(8,128)S(1)} %bitcast.301), channel_id=5, replica_groups=mesh['stream'=8,'girth'=4] {'stream'}, dimensions={0}, use_global_device_ids=true | all-gather | bytes 258048 | tf_op jit(solution)/shard_map/all_gather | solution.py:26
  172.1 11.0 %all-gather.11.cloned.1.call-done = f32[56,7,1024]{2,1,0:T(8,128)} async-done(((f32[7,7,1024]{2,1,0:T(8,128)}), f32[56,7,1024]{2,1,0:T(8,128)}) %all-gather.11.cloned.1.call-update) | async-done | bytes 1605648 | tf_op jit(solution)/shard_map/all_gather | solution.py:26
  183.1 8.7 %while.92 = (s32[]{:T(128)}, f32[7,1024]{1,0:T(8,128)S(1)}, s32[]{:T(128)}, f32[8,7,7,1024]{3,2,1,0:T(8,128)}, f32[8,7,1024]{2,1,0:T(8,128)S(1)}, /*index=5*/s32[]{:T(128)}, s32[]{:T(128)}, s32[]{:T(128)}, s32[]{:T(128)}) while((s32[]{:T(128)}, f32[7,1024]{1,0:T(8,128)S(1)}, s32[]{:T(128)}, f32[8,7,7,1024]{3,2,1,0:T(8,128)}, ...), condition=%wide.region_11.12_spmd.clone, body=%wide.region_10.11_spmd.clone.sunk | while | flops 121864 | bytes 430248 | solution.py:39
  183.1 1.0 fusion.129
  184.2 1.0 fusion.129
  185.3 1.0 fusion.129
  186.4 1.0 fusion.129
  187.5 1.0 fusion.129
  188.6 1.0 fusion.129
  189.6 1.0 fusion.129
  190.7 1.0 fusion.129
  (111 shorter events, 14.0 us)
Async XLA Ops:
  8.5 12.3 %all-to-all-start = ((s32[1,4,8]{2,0,1:T(1,128)}), s32[1,4,8]{2,0,1:T(1,128)S(1)}, u32[]{:S(2)}, u32[]{:S(2)}) async-start(s32[1,4,8]{2,0,1:T(1,128)} %bitcast.29), calls=%async_computation | async-start | bytes 4096 | tf_op jit(solution)/shard_map/all_to_all | solution.py:179
  20.8 8.9 %all-to-all-start.1 = ((f32[7,4,8]{0,2,1:T(8,128)}), f32[7,4,8]{0,2,1:T(8,128)S(1)}, u32[]{:S(2)}, u32[]{:S(2)}) async-start(f32[7,4,8]{0,2,1:T(8,128)} %fusion.49), calls=%async_computation.1 | async-start | bytes 32768 | tf_op jit(solution)/shard_map/all_to_all | solution.py:178
  25.0 86.6 %all-gather.9.cloned.1.call-start = ((), (), s32[]{:S(2)}) async-start(), calls=%async_computation.2 | async-start | bytes 2064384 | tf_op jit(solution)/shard_map/all_gather | solution.py:26
  31.8 5.6 %collective-permute-start = (f32[1,7,8,128]{3,1,2,0:T(8,128)S(1)}, f32[1,7,8,128]{3,1,2,0:T(8,128)S(1)}, u32[]{:S(2)}, u32[]{:S(2)}) collective-permute-start(f32[1,7,8,128]{3,1,2,0:T(8,128)S(1)} %get-tuple-element.730), channel_id=1, source_target_pairs={{0,4},{4,8},{8,12},{12,16},{16,20},{20,24},{24,28},{1,5},{5,9},{9,... | collective-permute-start | bytes 86024 | tf_op jit(solution)/shard_map/ppermute | solution.py:16
  33.2 5.2 %collective-permute-start.1 = (f32[1,7,8,128]{3,1,2,0:T(8,128)S(1)}, f32[1,7,8,128]{3,1,2,0:T(8,128)S(1)}, u32[]{:S(2)}, u32[]{:S(2)}) collective-permute-start(f32[1,7,8,128]{3,1,2,0:T(8,128)S(1)} %get-tuple-element.729), channel_id=1, source_target_pairs={{4,0},{8,4},{12,8},{16,12},{20,16},{24,20},{28,24},{5,1},{9,5},{13... | collective-permute-start | bytes 86024 | tf_op jit(solution)/shard_map/ppermute | solution.py:19
  34.5 4.8 %collective-permute-start.2 = (f32[2,7,1,128]{3,1,2,0:T(8,128)S(1)}, f32[2,7,1,128]{3,1,2,0:T(8,128)S(1)}, u32[]{:S(2)}, u32[]{:S(2)}) collective-permute-start(f32[2,7,1,128]{3,1,2,0:T(8,128)S(1)} %get-tuple-element.728), channel_id=1, source_target_pairs={{0,1},{1,2},{2,3},{3,0},{4,5},{5,6},{6,7},{7,4},{8,9},{9,10},{10,1... | collective-permute-start | bytes 21512 | tf_op jit(solution)/shard_map/ppermute | solution.py:16
  35.1 5.0 %collective-permute-start.3 = (f32[2,7,1,128]{3,1,2,0:T(8,128)S(1)}, f32[2,7,1,128]{3,1,2,0:T(8,128)S(1)}, u32[]{:S(2)}, u32[]{:S(2)}) collective-permute-start(f32[2,7,1,128]{3,1,2,0:T(8,128)S(1)} %get-tuple-element.727), channel_id=1, source_target_pairs={{1,0},{2,1},{3,2},{0,3},{5,4},{6,5},{7,6},{4,7},{9,8},{10,9},{11,1... | collective-permute-start | bytes 21512 | tf_op jit(solution)/shard_map/ppermute | solution.py:19
  49.1 3.4 %copy-start = (f32[7,7,1024]{0,1,2:T(8,128)S(1)}, f32[7,7,1024]{0,1,2:T(8,128)}, u32[]{:S(2)}) copy-start(f32[7,7,1024]{0,1,2:T(8,128)} %copy.110) | copy-start | bytes 602116 | tf_op jit(solution)/shard_map/while
  64.6 3.4 %copy-start = (f32[7,7,1024]{0,1,2:T(8,128)S(1)}, f32[7,7,1024]{0,1,2:T(8,128)}, u32[]{:S(2)}) copy-start(f32[7,7,1024]{0,1,2:T(8,128)} %copy.110) | copy-start | bytes 602116 | tf_op jit(solution)/shard_map/while
  76.4 3.5 %copy-start.3 = (f32[7,7]{1,0:T(8,128)S(1)}, f32[7,7]{1,0:T(8,128)}, u32[]{:S(2)}) copy-start(f32[7,7]{1,0:T(8,128)} %param.35) | copy-start | bytes 592
  76.4 43.7 %copy-start.2 = (f32[7,7]{1,0:T(8,128)S(1)}, f32[7,7]{1,0:T(8,128)}, u32[]{:S(2)}) copy-start(f32[7,7]{1,0:T(8,128)} %param.34) | copy-start | bytes 592
  79.9 103.3 %all-gather.11.cloned.1.call-start = ((), (), s32[]{:S(2)}) async-start(), calls=%async_computation.3 | async-start | bytes 2064384 | tf_op jit(solution)/shard_map/all_gather | solution.py:26
  126.2 3.4 %copy-start.1 = (f32[7,7,1024]{0,1,2:T(8,128)S(1)}, f32[7,7,1024]{0,1,2:T(8,128)}, u32[]{:S(2)}) copy-start(f32[7,7,1024]{0,1,2:T(8,128)} %copy.112) | copy-start | bytes 602116 | tf_op jit(solution)/shard_map/while
  141.3 3.4 %copy-start.1 = (f32[7,7,1024]{0,1,2:T(8,128)S(1)}, f32[7,7,1024]{0,1,2:T(8,128)}, u32[]{:S(2)}) copy-start(f32[7,7,1024]{0,1,2:T(8,128)} %copy.112) | copy-start | bytes 602116 | tf_op jit(solution)/shard_map/while
Sparse Core Ops, SparseCore 0:
  80.0 31.4 all-gather.8
  156.7 26.3 all-gather.10
where the time goes:
time: 201 us; the launch traced here: 200 us
  local copies, waits for them, and re-layouts  43.8 us (22%)
  matrix products  41.9 us (21%)
  blocking collectives  32.6 us (16%)
  waiting for transfers between devices  27.3 us (14%)
  other arithmetic  24 us (12%)
  starting transfers between devices  15 us (7%)
  between operations  14.3 us (7%)
    dot_general x4, matrix products, advance(): compound = jnp.einsum('ijc,jkc->ikc', factor, compound, precision=PRECISE)  33.3 us
    all_gather x2, blocking collectives, prefix(): everything = jax.tree.map(lambda part: lax.all_gather(part, axis), shard)  32.6 us
    all_gather x2, waiting for transfers between devices, prefix(): everything = jax.tree.map(lambda part: lax.all_gather(part, axis), shard)  24.6 us
    dot_general x16, other arithmetic, compose(): jnp.einsum('ijc,jc->ic', later_map[0], earlier[1], precision=PRECISE)  16.3 us
    while x12, local copies, waits for them, and re-layouts  13.8 us
    dot_general x4, local copies, waits for them, and re-layouts, advance(): factor = jnp.einsum('ijc,jk->ikc', block, matrix, precision=PRECISE)  10.7 us
    dot_general x6, matrix products, residual_from(): jnp.einsum('ij,ajbc->aibc', coupling[direction], beside[direction] - curr...  5.43 us
    all_to_all x1, starting transfers between devices, per_device(): lax.all_to_all(target, 'girth', split_axis=1, concat_axis=1, tiled=True)  5.16 us
  transfers between devices with their start and end apart: 8, of which 3 were waited for; matrix products, arithmetic and copies ran while one was open for 6% of the time, Pallas kernels for 0%

commit v1 on v0

v1 whole, which is shorter than its diff:
```python
import functools

import jax
import jax.numpy as jnp
from jax import lax
from jax.experimental import pallas as pl
from jax.experimental.pallas import tpu as pltpu
from jax.sharding import PartitionSpec as P

MESH = pl.DeviceIdType.MESH
PRECISE = lax.Precision.HIGHEST
VARS = 7
ROWS = 2
TEAM = 4
PAIR = 2
CAP = 8


def kernel(
    n_stream,
    n_girth,
    state,
    prop,
    donor,
    landing,
    weight,
    disk,
    thrust,
    face,
    coupling,
    inverse,
    lower,
    upper,
    new_state,
    residual_out,
    packet,
    packets,
    edge_out,
    edge_in,
    row_in,
    planes,
    inv_out,
    inv_in,
    current,
    rhs_planes,
    rhs_out,
    rhs_in,
    fmap,
    bmap,
    upd_out,
    upd_in,
    link_out,
    link_in,
    packet_sems,
    edge_sems,
    row_sems,
    inv_sems,
    rhs_sems,
    upd_sems,
    link_sems,
    local_sems,
):
    s, g = lax.axis_index("stream"), lax.axis_index("girth")
    base = (s // TEAM) * TEAM
    place = s - base
    team = s // TEAM
    n_teams = n_stream // TEAM
    slots = donor.shape[1]
    packs = n_girth if n_girth * slots <= 128 else 1

    def girth_at(k):
        return lax.rem(g + k + n_girth, n_girth)

    def remote(src, dst, sems, at, to):
        return pltpu.make_async_remote_copy(
            src_ref=src,
            dst_ref=dst,
            send_sem=sems.at[(0, *at)],
            recv_sem=sems.at[(1, *at)],
            device_id=to,
            device_id_type=MESH,
        )

    def has(ds):
        return jnp.logical_and(s + ds >= 0, s + ds < n_stream)

    barrier = pltpu.get_barrier_semaphore()

    def greet(to):
        pl.semaphore_signal(barrier, inc=1, device_id=to, device_id_type=MESH)

    for k in range(1, n_girth):
        greet((s, girth_at(k)))
    expected = n_girth - 1
    for ds in (-1, 1):

        @pl.when(has(ds))
        def _():
            for k in range(n_girth):
                greet((s + ds, girth_at(k)))

        expected = expected + jnp.where(has(ds), n_girth, 0)
    for k in range(1, TEAM):
        q = lax.rem(place + k, TEAM)
        far = jnp.logical_or(q - place > 1, place - q > 1)

        @pl.when(far)
        def _():
            greet((base + q, g))

        expected = expected + jnp.where(far, 1, 0)
    for ds in (-TEAM, TEAM):

        @pl.when(has(ds))
        def _():
            greet((s + ds, g))

        expected = expected + jnp.where(has(ds), 1, 0)

    lane = lax.broadcasted_iota(jnp.int32, (1, 128), 1)

    def spread(ref):
        return jnp.concatenate([ref[...]] * packs, axis=1) if packs > 1 else ref[...]

    donor_all = spread(donor)
    live = jnp.logical_and(lane // slots == lax.rem(g, packs), donor_all >= 0)
    cell = lax.broadcasted_iota(jnp.int32, (prop.shape[1], 128), 0)
    chosen = jnp.where(cell == jnp.where(live, donor_all, -1), 1.0, 0.0)
    taken = jnp.dot(prop[...], chosen, precision=PRECISE, preferred_element_type=jnp.float32)
    packet[0:VARS, :] = taken * jnp.where(live, spread(weight), 0.0)
    packet[VARS : VARS + 1, :] = jnp.where(live, spread(landing) + 1, 0).astype(jnp.float32)
    packets[1, 0] = packet[...]

    for side, at in ((0, 0), (1, 7)):
        for r in range(ROWS):
            edge_out[side, r, 0:VARS, :] = state[pl.ds(r * VARS * 8 + at, VARS, stride=8), :]
            edge_out[side, r, VARS : VARS + 1, :] = jnp.zeros((1, 128), jnp.float32)

    pl.semaphore_wait(barrier, expected)

    def packet_copy(ds, k):
        return remote(
            packet, packets.at[1 - ds, k], packet_sems, (1 - ds, k), (s + ds, girth_at(k))
        )

    def edge_copy(side):
        return remote(
            edge_out.at[side], edge_in.at[side], edge_sems, (side,), (s, girth_at(2 * side - 1))
        )

    def row_copy(side):
        rows = VARS * 8
        return remote(
            state.at[pl.ds(side * rows, rows)],
            row_in.at[side],
            row_sems,
            (side,),
            (s + 2 * side - 1, g),
        )

    for ds in (-1, 1):

        @pl.when(has(ds))
        def _():
            row_copy((ds + 1) // 2).start()
            for k in range(n_girth):
                packet_copy(ds, k).start()

    for side in (0, 1):
        edge_copy(side).start()
    for k in range(1, n_girth):
        packet_copy(0, k).start()

    for r in range(ROWS):
        for i in range(VARS):
            for j in range(VARS):
                p = (r * VARS + i) * VARS + j
                planes[p * 8 : p * 8 + 8, :] = inverse[r, i, j].astype(jnp.float32)
    blocks = planes.shape[0] // 64
    planes[ROWS * VARS * VARS * 8 :, :] = jnp.zeros(
        (planes.shape[0] - ROWS * VARS * VARS * 8, 128), jnp.float32
    )
    for c in range(8):
        for b in range(blocks):
            inv_out[c // PAIR, c % PAIR, b * 8 : b * 8 + 8, :] = planes[
                pl.ds(b * 64 + c, 8, stride=8), :
            ]

    def team_copy(out, into, sems, k):
        q = lax.rem(place + k, TEAM)
        return remote(out.at[q], into.at[place], sems, (k,), (base + q, g))

    def own_copy(out, into, n):
        return pltpu.make_async_copy(out.at[place], into.at[place], local_sems.at[n])

    for k in range(1, TEAM):
        team_copy(inv_out, inv_in, inv_sems, k).start()
    own_copy(inv_out, inv_in, 0).start()

    for side in (0, 1):
        edge_copy(side).wait_recv()
    for k in range(1, n_girth):
        packet_copy(0, k).wait_recv()
    for ds in (-1, 1):

        @pl.when(has(ds))
        def _():
            row_copy((1 - ds) // 2).wait_recv()
            for k in range(n_girth):
                packet_copy(-ds, k).wait_recv()

    girth_cell = lax.broadcasted_iota(jnp.int32, (8, 128), 0)
    normal_cell = lax.broadcasted_iota(jnp.int32, (8, 128), 1)
    normal_rows = lax.broadcasted_iota(jnp.int32, (128, 128), 0)
    var_row = lax.broadcasted_iota(jnp.int32, (8, 128), 0)
    peer = lax.rem(lane, slots) // CAP

    def landed(o, plan):
        total = None
        for first in range(0, n_girth, packs):
            tile = packets[o, first]
            for k in range(first + 1, first + packs):
                tile = tile + packets[o, k]
            code = tile[VARS : VARS + 1, :].astype(jnp.int32) - 1
            row, gc, nc = code >> 10, (code >> 7) & 7, code & 127
            nc = jnp.where(code >= 0, nc, -1)
            tile = jnp.where(var_row == VARS, 1.0, tile)
            part = lax.dot_general(
                jnp.concatenate(plan(tile, row, gc), axis=0),
                jnp.where(normal_rows == nc, 1.0, 0.0),
                (((1,), (1,)), ((), ())),
                precision=PRECISE,
                preferred_element_type=jnp.float32,
            )
            total = part if total is None else total + part
        return total

    def block_rows(r):
        def plan(tile, row, gc):
            here = jnp.logical_and(row == r, peer == g)
            hit = jnp.where(girth_cell == jnp.where(here, gc, -1), 1.0, 0.0)
            return [tile[v : v + 1, :] * hit for v in range(8)]

        return plan

    def own_plan(tile, row, gc):
        rows = block_rows(0)(tile, row, gc) + block_rows(1)(tile, row, gc)
        for at, side in ((7, -1), (0, 1)):
            for r in range(ROWS):
                here = (peer == girth_at(side)) & (row == r) & (gc == at)
                rows.append(tile * jnp.where(here, 1.0, 0.0))
        return rows

    def settle(found, raw):
        hit = found[VARS * 8 : VARS * 8 + 8] > 0.5
        return [jnp.where(hit, found[v * 8 : v * 8 + 8], raw(v)) for v in range(VARS)], hit

    own = landed(1, own_plan)
    cells, fringe = [], []
    for r in range(ROWS):
        found, hit = settle(
            own[r * 64 : r * 64 + 64], lambda v: state[(r * VARS + v) * 8 : (r * VARS + v) * 8 + 8, :]
        )
        cells.append(found)
        fringe.append(hit)
        for v in range(VARS):
            current[(r * VARS + v) * 8 : (r * VARS + v) * 8 + 8, :] = found[v]
    beside = {}
    for side in (0, 1):
        for r in range(ROWS):
            at = 128 + (side * ROWS + r) * 8
            found = own[at : at + 8]
            beside[side, r] = jnp.where(
                found[VARS : VARS + 1] > 0.5, found, edge_in[1 - side, r]
            )
    outer = []
    for o, r, side in ((0, 1, 1), (2, 0, 0)):
        found, _ = settle(
            landed(o, block_rows(r)), lambda v: row_in[side, v * 8 : v * 8 + 8, :]
        )
        outer.append([jnp.where(has(o - 1), x, 0.0) for x in found])

    for r in range(ROWS):
        here = cells[r]
        before = outer[0] if r == 0 else cells[r - 1]
        after = outer[1] if r == ROWS - 1 else cells[r + 1]
        in_disk = disk[r * 8 : r * 8 + 8, :].astype(jnp.float32)
        total = [in_disk * thrust[v] for v in range(VARS)]
        for d in range(6):
            step = []
            for v in range(VARS):
                x = here[v]
                if d == 0:
                    near = before[v]
                elif d == 1:
                    near = after[v]
                elif d == 2:
                    near = jnp.where(girth_cell == 0, beside[0, r][v : v + 1], pltpu.roll(x, 1, 0))
                elif d == 3:
                    near = jnp.where(girth_cell == 7, beside[1, r][v : v + 1], pltpu.roll(x, 7, 0))
                elif d == 4:
                    near = jnp.where(normal_cell == 0, 0.0, pltpu.roll(x, 1, 1))
                else:
                    near = jnp.where(normal_cell == 127, 0.0, pltpu.roll(x, 127, 1))
                step.append(near - x)
            area = face[(r * 6 + d) * 8 : (r * 6 + d) * 8 + 8, :]
            for i in range(VARS):
                flux = step[0] * coupling[d, i, 0]
                for j in range(1, VARS):
                    flux = flux + step[j] * coupling[d, i, j]
                total[i] = total[i] + area * flux
        for v in range(VARS):
            residual_out[(r * VARS + v) * 8 : (r * VARS + v) * 8 + 8, :] = total[v]
            rhs_planes[r, v * 8 : v * 8 + 8, :] = jnp.where(fringe[r], 0.0, -total[v])
        for c in range(8):
            rhs_out[c // PAIR, r, c % PAIR, 0:VARS, :] = rhs_planes[r, pl.ds(c, VARS, stride=8), :]

    for k in range(1, TEAM):
        team_copy(rhs_out, rhs_in, rhs_sems, k).start()
    own_copy(rhs_out, rhs_in, 1).start()

    for k in range(1, TEAM):
        team_copy(inv_out, inv_in, inv_sems, TEAM - k).wait_send()
        pltpu.make_async_remote_copy(
            src_ref=inv_out.at[place],
            dst_ref=inv_in.at[lax.rem(place + TEAM - k, TEAM)],
            send_sem=inv_sems.at[0, k],
            recv_sem=inv_sems.at[1, k],
            device_id=(base + lax.rem(place + k, TEAM), g),
            device_id_type=MESH,
        ).wait_recv()
    own_copy(inv_out, inv_in, 0).wait()

    def column(k, h, r, j):
        return inv_in[k, h, pl.ds(r * VARS * VARS + j, VARS, stride=VARS), :]

    def matrices(k, carry):
        for r in range(ROWS):
            for h in range(PAIR):
                cols = [column(k, h, r, j) for j in range(VARS)]
                for m in range(VARS):
                    f, b = cols[0] * lower[0, m], cols[0] * upper[0, m]
                    for j in range(1, VARS):
                        f = f + cols[j] * lower[j, m]
                        b = b + cols[j] * upper[j, m]
                    fmap[k, r, h, m, 0:VARS, :] = f
                    bmap[k, r, h, m, 0:VARS, :] = b
        return carry

    lax.fori_loop(0, TEAM, matrices, 0)

    for k in range(1, TEAM):
        team_copy(rhs_out, rhs_in, rhs_sems, TEAM - k).wait_send()
        pltpu.make_async_remote_copy(
            src_ref=rhs_out.at[place],
            dst_ref=rhs_in.at[lax.rem(place + TEAM - k, TEAM)],
            send_sem=rhs_sems.at[0, k],
            recv_sem=rhs_sems.at[1, k],
            device_id=(base + lax.rem(place + k, TEAM), g),
            device_id_type=MESH,
        ).wait_recv()
    own_copy(rhs_out, rhs_in, 1).wait()

    def product(matrix, x):
        parts = [matrix(j) * x[j : j + 1, :] for j in range(VARS)]
        return ((parts[0] + parts[1]) + (parts[2] + parts[3])) + (
            (parts[4] + parts[5]) + parts[6]
        )

    offsets = {}
    for k in range(TEAM):
        for r in range(ROWS):
            for h in range(PAIR):
                offsets[k, r, h] = product(
                    lambda j: column(k, h, r, j), rhs_in[k, r, h, 0:VARS, :]
                )

    def link_copy(way):
        return remote(
            link_out.at[way], link_in.at[way], link_sems, (way,), (s + (1 - 2 * way) * TEAM, g)
        )

    def arrive(way, there):
        @pl.when(there)
        def _():
            link_copy(way).wait_recv()

        return [jnp.where(there, link_in[way, h, 0:VARS, :], 0.0) for h in range(PAIR)]

    def depart(way, there, x):
        for h in range(PAIR):
            link_out[way, h, 0:VARS, :] = x[h]

        @pl.when(there)
        def _():
            link_copy(way).start()

    def upd_copy(k):
        q = lax.rem(place + k, TEAM)
        return remote(
            upd_out.at[q],
            upd_in.at[:, pl.ds(pl.multiple_of(place * PAIR * 8, PAIR * 8), PAIR * 8)],
            upd_sems,
            (k,),
            (base + q, g),
        )

    x = arrive(0, team > 0)
    stars = {}
    for k in range(TEAM):
        for r in range(ROWS):
            for h in range(PAIR):
                x[h] = offsets[k, r, h] + product(
                    lambda m: fmap[k, r, h, m, 0:VARS, :], x[h]
                )
                stars[k, r, h] = x[h]
    depart(0, team < n_teams - 1, x)
    x = arrive(1, team < n_teams - 1)
    for k in reversed(range(TEAM)):
        for r in reversed(range(ROWS)):
            for h in range(PAIR):
                x[h] = stars[k, r, h] + product(lambda m: bmap[k, r, h, m, 0:VARS, :], x[h])
                upd_out[k, r, h * 8 : h * 8 + VARS, :] = x[h]
    depart(1, team > 0, x)
    for k in range(1, TEAM):
        upd_copy(k).start()
    own = pltpu.make_async_copy(
        upd_out.at[place],
        upd_in.at[:, pl.ds(pl.multiple_of(place * PAIR * 8, PAIR * 8), PAIR * 8)],
        local_sems.at[2],
    )
    own.start()
    own.wait()
    for k in range(1, TEAM):
        q = lax.rem(place + TEAM - k, TEAM)
        pltpu.make_async_remote_copy(
            src_ref=upd_out.at[place],
            dst_ref=upd_in.at[:, pl.ds(pl.multiple_of(q * PAIR * 8, PAIR * 8), PAIR * 8)],
            send_sem=upd_sems.at[0, k],
            recv_sem=upd_sems.at[1, k],
            device_id=(base + lax.rem(place + k, TEAM), g),
            device_id_type=MESH,
        ).wait_recv()
    for r in range(ROWS):
        for v in range(VARS):
            at = (r * VARS + v) * 8
            new_state[at : at + 8, :] = current[at : at + 8, :] + upd_in[r, pl.ds(v, 8, stride=8), :]

    for k in range(1, TEAM):
        upd_copy(k).wait_send()
    for side in (0, 1):
        edge_copy(side).wait_send()
    for k in range(1, n_girth):
        packet_copy(0, k).wait_send()
    for ds in (-1, 1):

        @pl.when(has(ds))
        def _():
            row_copy((ds + 1) // 2).wait_send()
            for k in range(n_girth):
                packet_copy(ds, k).wait_send()

    for way, there in ((0, team < n_teams - 1), (1, team > 0)):

        @pl.when(there)
        def _():
            link_copy(way).wait_send()


def per_device(
    state,
    propeller,
    donor_index,
    fringe_index,
    donor_weight,
    disk_mask,
    thrust,
    face,
    coupling,
    diag_inverse,
    lower_jacobian,
    upper_jacobian,
):
    n_stream, n_girth = lax.axis_size("stream"), lax.axis_size("girth")
    f32 = jnp.float32
    vmem = pl.BlockSpec(memory_space=pltpu.VMEM)
    smem = pl.BlockSpec(memory_space=pltpu.SMEM)
    blocks = ROWS * VARS * 8
    padded = -(-ROWS * VARS * VARS // 8) * 8
    dma = pltpu.SemaphoreType.DMA
    new_state, residual = pl.pallas_call(
        functools.partial(kernel, n_stream, n_girth),
        out_shape=[jax.ShapeDtypeStruct((blocks, 128), f32)] * 2,
        in_specs=[vmem] * 6 + [smem, vmem, smem, vmem, smem, smem],
        out_specs=[vmem, vmem],
        scratch_shapes=[
            pltpu.VMEM((8, 128), f32),
            pltpu.VMEM((3, n_girth, 8, 128), f32),
            pltpu.VMEM((2, ROWS, 8, 128), f32),
            pltpu.VMEM((2, ROWS, 8, 128), f32),
            pltpu.VMEM((2, VARS * 8, 128), f32),
            pltpu.VMEM((padded * 8, 128), f32),
            pltpu.VMEM((TEAM, PAIR, padded, 128), f32),
            pltpu.VMEM((TEAM, PAIR, padded, 128), f32),
            pltpu.VMEM((blocks, 128), f32),
            pltpu.VMEM((ROWS, VARS * 8, 128), f32),
            pltpu.VMEM((TEAM, ROWS, PAIR, 8, 128), f32),
            pltpu.VMEM((TEAM, ROWS, PAIR, 8, 128), f32),
            pltpu.VMEM((TEAM, ROWS, PAIR, VARS, 8, 128), f32),
            pltpu.VMEM((TEAM, ROWS, PAIR, VARS, 8, 128), f32),
            pltpu.VMEM((TEAM, ROWS, PAIR * 8, 128), f32),
            pltpu.VMEM((ROWS, TEAM * PAIR * 8, 128), f32),
            pltpu.VMEM((2, PAIR, 8, 128), f32),
            pltpu.VMEM((2, PAIR, 8, 128), f32),
            dma((2, 3, n_girth)),
            dma((2, 2)),
            dma((2, 2)),
            dma((2, TEAM)),
            dma((2, TEAM)),
            dma((2, TEAM)),
            dma((2, 2)),
            dma((3,)),
        ],
        compiler_params=pltpu.CompilerParams(
            collective_id=0, has_side_effects=True, vmem_limit_bytes=24 * 1024 * 1024
        ),
        cost_estimate=pl.CostEstimate(flops=12_000_000, bytes_accessed=500_000, transcendentals=0),
    )(
        state.reshape(blocks, 128),
        propeller,
        donor_index,
        fringe_index,
        donor_weight,
        disk_mask.reshape(ROWS * 8, 128),
        thrust,
        face.reshape(ROWS * 6 * 8, 128),
        coupling,
        diag_inverse,
        lower_jacobian,
        upper_jacobian,
    )
    return new_state.reshape(state.shape), residual.reshape(state.shape)


def solution(mesh):
    placed = (
        P("stream", None, "girth", None),
        P(None, ("stream", "girth")),
        P(("stream", "girth"), None),
        P(("stream", "girth"), None),
        P(("stream", "girth"), None),
        P("stream", "girth", None),
        P(),
        P("stream", None, "girth", None),
        P(),
        P("stream", None, None, "girth", None),
        P(),
        P(),
    )
    return jax.shard_map(
        per_device,
        mesh=mesh,
        in_specs=placed,
        out_specs=(P("stream", None, "girth", None), P("stream", None, "girth", None)),
        check_vma=False,
    )
```

time: 201 us -> 32.5 us (0.16)
  matrix products: 41.9 us -> 0 us
  local copies, waits for them, and re-layouts: 43.8 us -> 7.93 us
  blocking collectives: 32.6 us -> 0 us
  waiting for transfers between devices: 27.3 us -> 0 us
  other arithmetic: 24 us -> 0 us
  Pallas kernels: 0 us -> 23.4 us
  starting transfers between devices: 15 us -> 0 us
  between operations: 14.3 us -> 0.69 us
    dot_general x22 -> x0, matrix products: 41.9 us -> none  [the longest x4 33.3 us: advance(): compound = jnp.einsum('ijc,jkc->ikc', factor, compound, precision=PRECISE)]
    all_gather x2 -> x0, blocking collectives: 32.6 us -> none  [prefix(): everything = jax.tree.map(lambda part: lax.all_gather(part, axis), shard)]
    all_gather x2 -> x0, waiting for transfers between devices: 24.6 us -> none  [prefix(): everything = jax.tree.map(lambda part: lax.all_gather(part, axis), shard)]
    pallas_call x0 -> x1, Pallas kernels: none -> 23.4 us  [per_device(): pl.pallas_call(functools.partial(kernel, n_stream, n_girth), out_shape=[j...]
    while x16 -> x0, local copies, waits for them, and re-layouts: 21.6 us -> none
    dot_general x22 -> x0, other arithmetic: 16.8 us -> none  [the longest x16 16.3 us: compose(): jnp.einsum('ijc,jc->ic', later_map[0], earlier[1], precision=PRECISE)]
    dot_general x6 -> x0, local copies, waits for them, and re-layouts: 11.2 us -> none  [the longest x4 10.7 us: advance(): factor = jnp.einsum('ijc,jk->ikc', block, matrix, precision=PRECISE)]
    all_to_all x2 -> x0, starting transfers between devices: 9.36 us -> none  [the longest x1 5.16 us: per_device(): lax.all_to_all(target, 'girth', split_axis=1, concat_axis=1, tiled=True)]
  transfers between devices with their start and end apart: 8 -> 0, of which waited for: 3 -> 0; matrix products, arithmetic and copies ran while one was open for 6% -> 0% of each run, Pallas kernels for 0% -> 0%
where the time goes in v1:
time: 32.5 us; the launch traced here: 32.1 us
  Pallas kernels  23.4 us (72%)
  local copies, waits for them, and re-layouts  7.93 us (24%)
  between operations  0.69 us (2%)
    pallas_call x1, Pallas kernels, per_device(): pl.pallas_call(functools.partial(kernel, n_stream, n_girth), out_shape=[j...  23.4 us
    unnamed x26, local copies, waits for them, and re-layouts  7.93 us

profile of v1, /device:TPU:0, one launch (start us, length us, event | category | flops | bytes accessed | tf_op | source)
XLA Modules:
  0.0 32.1 jit_solution(10393080963348047943)
XLA Ops:
  0.6 0.0 copy-start.6
  0.6 0.0 copy-start.8
  0.7 0.0 copy-start.9
  0.7 0.0 copy-start.10
  0.7 0.6 %copy-done.6 = f32[7,7]{1,0:T(8,128)S(1)} copy-done((f32[7,7]{1,0:T(8,128)S(1)}, f32[7,7]{1,0:T(8,128)}, u32[]{:S(2)}) %copy-start.6) | copy-done | bytes 220
  1.3 0.0 copy-done.8
  1.3 0.0 copy-done.9
  1.3 0.0 copy-done.10
  1.3 0.0 copy-start
  1.3 0.9 %copy-done = bf16[2,7,7,8,128]{4,3,2,1,0:T(8,128)(2,1)S(1)} copy-done((bf16[2,7,7,8,128]{4,3,2,1,0:T(8,128)(2,1)S(1)}, bf16[2,7,7,8,128]{4,3,2,1,0:T(8,128)(2,1)}, u32[]{:S(2)}) %copy-start) | copy-done | bytes 200728
  2.3 0.0 copy-start.1
  2.3 0.8 %copy-done.1 = f32[2,7,8,128]{3,2,1,0:T(8,128)S(1)} copy-done((f32[2,7,8,128]{3,2,1,0:T(8,128)S(1)}, f32[2,7,8,128]{3,2,1,0:T(8,128)}, u32[]{:S(2)}) %copy-start.1) | copy-done | bytes 57368
  3.1 0.0 copy-start.2
  3.1 0.8 %copy-done.2 = f32[2,6,8,128]{3,2,1,0:T(8,128)S(1)} copy-done((f32[2,6,8,128]{3,2,1,0:T(8,128)S(1)}, f32[2,6,8,128]{3,2,1,0:T(8,128)}, u32[]{:S(2)}) %copy-start.2) | copy-done | bytes 49176
  3.9 0.0 copy-start.3
  3.9 0.7 %copy-done.3 = f32[6,7,7]{2,1,0:T(8,128)S(1)} copy-done((f32[6,7,7]{2,1,0:T(8,128)S(1)}, f32[6,7,7]{2,1,0:T(8,128)}, u32[]{:S(2)}) %copy-start.3) | copy-done | bytes 1200
  4.6 0.0 copy-start.4
  4.6 0.7 %copy-done.4 = f32[7,256]{1,0:T(8,128)S(1)} copy-done((f32[7,256]{1,0:T(8,128)S(1)}, f32[7,256]{1,0:T(8,128)}, u32[]{:S(2)}) %copy-start.4) | copy-done | bytes 7192
  5.3 0.0 copy-start.5
  5.3 0.7 %copy-done.5 = s32[2,8,128]{2,1,0:T(8,128)S(1)} copy-done((s32[2,8,128]{2,1,0:T(8,128)S(1)}, s32[2,8,128]{2,1,0:T(8,128)}, u32[]{:S(2)}) %copy-start.5) | copy-done | bytes 8216
  6.0 0.0 copy-start.7
  6.0 0.7 %copy-done.7 = f32[7,7]{1,0:T(8,128)S(1)} copy-done((f32[7,7]{1,0:T(8,128)S(1)}, f32[7,7]{1,0:T(8,128)}, u32[]{:S(2)}) %copy-start.7) | copy-done | bytes 220
  6.7 0.0 copy-start.11
  6.7 0.7 %copy-done.11 = f32[7]{0:T(128)S(1)} copy-done((f32[7]{0:T(128)S(1)}, f32[7]{0:T(128)}, u32[]{:S(2)}) %copy-start.11) | copy-done | bytes 52
  7.4 23.4 %shard_map.131 = (f32[112,128]{1,0:T(8,128)S(1)}, f32[112,128]{1,0:T(8,128)S(1)}) custom-call(f32[112,128]{1,0:T(8,128)S(1)} %bitcast.7, f32[7,256]{1,0:T(8,128)S(1)} %copy-done.4, s32[1,32]{1,0:T(1,128)S(1)} %copy-done.8, s32[1,32]{1,0:T(1,128)S(1)} %copy-done.9, f32[1,32]{1,0:T(1,128)S(1)} %copy-done.10, s32[16,128]{1,0:T(8,128)S(1)} %bitcast.9, ...), custom_call_target="tpu_custom_call" | custom-call | flops 12000000 | bytes 500000 | tf_op jit(solution)/shard_map/pallas_call | solution.py:491
  30.8 0.6 %copy.16 = f32[2,7,8,128]{3,2,1,0:T(8,128)} copy(f32[2,7,8,128]{3,2,1,0:T(8,128)S(1)} %bitcast.6) | data formatting | bytes 114688
  31.4 0.6 %copy.17 = f32[2,7,8,128]{3,2,1,0:T(8,128)} copy(f32[2,7,8,128]{3,2,1,0:T(8,128)S(1)} %bitcast.5) | data formatting | bytes 114688
Async XLA Ops:
  0.6 0.7 %copy-start.6 = (f32[7,7]{1,0:T(8,128)S(1)}, f32[7,7]{1,0:T(8,128)}, u32[]{:S(2)}) copy-start(f32[7,7]{1,0:T(8,128)} %lower.1) | copy-start | bytes 592
  0.6 0.7 %copy-start.8 = (s32[1,32]{1,0:T(1,128)S(1)}, s32[1,32]{1,0:T(1,128)}, u32[]{:S(2)}) copy-start(s32[1,32]{1,0:T(1,128)} %donor.1) | copy-start | bytes 388
  0.7 0.7 %copy-start.9 = (s32[1,32]{1,0:T(1,128)S(1)}, s32[1,32]{1,0:T(1,128)}, u32[]{:S(2)}) copy-start(s32[1,32]{1,0:T(1,128)} %landing.1) | copy-start | bytes 388
  0.7 0.7 %copy-start.10 = (f32[1,32]{1,0:T(1,128)S(1)}, f32[1,32]{1,0:T(1,128)}, u32[]{:S(2)}) copy-start(f32[1,32]{1,0:T(1,128)} %weight.1) | copy-start | bytes 388
  1.3 0.9 %copy-start = (bf16[2,7,7,8,128]{4,3,2,1,0:T(8,128)(2,1)S(1)}, bf16[2,7,7,8,128]{4,3,2,1,0:T(8,128)(2,1)}, u32[]{:S(2)}) copy-start(bf16[2,7,7,8,128]{4,3,2,1,0:T(8,128)(2,1)} %inverse.1) | copy-start | bytes 602116
  2.3 0.8 %copy-start.1 = (f32[2,7,8,128]{3,2,1,0:T(8,128)S(1)}, f32[2,7,8,128]{3,2,1,0:T(8,128)}, u32[]{:S(2)}) copy-start(f32[2,7,8,128]{3,2,1,0:T(8,128)} %param.12) | copy-start | bytes 172036
  3.1 0.8 %copy-start.2 = (f32[2,6,8,128]{3,2,1,0:T(8,128)S(1)}, f32[2,6,8,128]{3,2,1,0:T(8,128)}, u32[]{:S(2)}) copy-start(f32[2,6,8,128]{3,2,1,0:T(8,128)} %param.19) | copy-start | bytes 147460
  3.9 0.7 %copy-start.3 = (f32[6,7,7]{2,1,0:T(8,128)S(1)}, f32[6,7,7]{2,1,0:T(8,128)}, u32[]{:S(2)}) copy-start(f32[6,7,7]{2,1,0:T(8,128)} %coupling.1) | copy-start | bytes 3532
  4.6 0.7 %copy-start.4 = (f32[7,256]{1,0:T(8,128)S(1)}, f32[7,256]{1,0:T(8,128)}, u32[]{:S(2)}) copy-start(f32[7,256]{1,0:T(8,128)} %prop.1) | copy-start | bytes 21508
  5.3 0.7 %copy-start.5 = (s32[2,8,128]{2,1,0:T(8,128)S(1)}, s32[2,8,128]{2,1,0:T(8,128)}, u32[]{:S(2)}) copy-start(s32[2,8,128]{2,1,0:T(8,128)} %param.17) | copy-start | bytes 24580
  6.0 0.7 %copy-start.7 = (f32[7,7]{1,0:T(8,128)S(1)}, f32[7,7]{1,0:T(8,128)}, u32[]{:S(2)}) copy-start(f32[7,7]{1,0:T(8,128)} %upper.1) | copy-start | bytes 592
  6.7 0.7 %copy-start.11 = (f32[7]{0:T(128)S(1)}, f32[7]{0:T(128)}, u32[]{:S(2)}) copy-start(f32[7]{0:T(128)} %thrust.1) | copy-start | bytes 88

commit v2 on v1

--- a/solution.py
+++ b/solution.py
@@ -19,47 +19,43 @@
 def kernel(
     n_stream,
     n_girth,
-    state,
-    prop,
-    donor,
-    landing,
-    weight,
-    disk,
-    thrust,
-    face,
-    coupling,
-    inverse,
-    lower,
-    upper,
-    new_state,
-    residual_out,
-    packet,
-    packets,
-    edge_out,
-    edge_in,
-    row_in,
-    planes,
-    inv_out,
-    inv_in,
-    current,
-    rhs_planes,
-    rhs_out,
-    rhs_in,
-    fmap,
-    bmap,
-    upd_out,
-    upd_in,
-    link_out,
-    link_in,
-    packet_sems,
-    edge_sems,
-    row_sems,
-    inv_sems,
-    rhs_sems,
-    upd_sems,
-    link_sems,
-    local_sems,
+    *refs,
 ):
+    given, results, held = refs[:12], refs[12:14], refs[14:26]
+    state, prop, donor, landing, weight, disk = held[:6]
+    thrust, face, coupling, inverse, lower, upper = held[6:]
+    (
+        new_state,
+        residual_out,
+        packet,
+        packets,
+        edge_out,
+        edge_in,
+        row_in,
+        planes,
+        inv_out,
+        inv_in,
+        current,
+        rhs_planes,
+        rhs_out,
+        rhs_in,
+        fmap,
+        bmap,
+        upd_out,
+        upd_in,
+        link_out,
+        link_in,
+        packet_sems,
+        edge_sems,
+        row_sems,
+        inv_sems,
+        rhs_sems,
+        upd_sems,
+        link_sems,
+        local_sems,
+        load_sems,
+        store_sems,
+    ) = refs[26:]
     s, g = lax.axis_index("stream"), lax.axis_index("girth")
     base = (s // TEAM) * TEAM
     place = s - base
@@ -84,6 +80,12 @@
     def has(ds):
         return jnp.logical_and(s + ds >= 0, s + ds < n_stream)
 
+    def load(n):
+        return pltpu.make_async_copy(given[n], held[n], load_sems.at[n])
+
+    for n in (2, 3, 4, 1, 0, 9, 7, 8, 5, 6, 10, 11):
+        load(n).start()
+
     barrier = pltpu.get_barrier_semaphore()
 
     def greet(to):
@@ -116,6 +118,9 @@
             greet((s + ds, g))
 
         expected = expected + jnp.where(has(ds), 1, 0)
+
+    for n in (1, 2, 3, 4):
+        load(n).wait()
 
     lane = lax.broadcasted_iota(jnp.int32, (1, 128), 1)
 
@@ -131,46 +136,13 @@
     packet[VARS : VARS + 1, :] = jnp.where(live, spread(landing) + 1, 0).astype(jnp.float32)
     packets[1, 0] = packet[...]
 
+    load(0).wait()
     for side, at in ((0, 0), (1, 7)):
         for r in range(ROWS):
             edge_out[side, r, 0:VARS, :] = state[pl.ds(r * VARS * 8 + at, VARS, stride=8), :]
             edge_out[side, r, VARS : VARS + 1, :] = jnp.zeros((1, 128), jnp.float32)
 
-    pl.semaphore_wait(barrier, expected)
-
-    def packet_copy(ds, k):
-        return remote(
-            packet, packets.at[1 - ds, k], packet_sems, (1 - ds, k), (s + ds, girth_at(k))
-        )
-
-    def edge_copy(side):
-        return remote(
-            edge_out.at[side], edge_in.at[side], edge_sems, (side,), (s, girth_at(2 * side - 1))
-        )
-
-    def row_copy(side):
-        rows = VARS * 8
-        return remote(
-            state.at[pl.ds(side * rows, rows)],
-            row_in.at[side],
-            row_sems,
-            (side,),
-            (s + 2 * side - 1, g),
-        )
-
-    for ds in (-1, 1):
-
-        @pl.when(has(ds))
-        def _():
-            row_copy((ds + 1) // 2).start()
-            for k in range(n_girth):
-                packet_copy(ds, k).start()
-
-    for side in (0, 1):
-        edge_copy(side).start()
-    for k in range(1, n_girth):
-        packet_copy(0, k).start()
-
+    load(9).wait()
     for r in range(ROWS):
         for i in range(VARS):
             for j in range(VARS):
@@ -185,6 +157,41 @@
             inv_out[c // PAIR, c % PAIR, b * 8 : b * 8 + 8, :] = planes[
                 pl.ds(b * 64 + c, 8, stride=8), :
             ]
+
+    pl.semaphore_wait(barrier, expected)
+
+    def packet_copy(ds, k):
+        return remote(
+            packet, packets.at[1 - ds, k], packet_sems, (1 - ds, k), (s + ds, girth_at(k))
+        )
+
+    def edge_copy(side):
+        return remote(
+            edge_out.at[side], edge_in.at[side], edge_sems, (side,), (s, girth_at(2 * side - 1))
+        )
+
+    def row_copy(side):
+        rows = VARS * 8
+        return remote(
+            state.at[pl.ds(side * rows, rows)],
+            row_in.at[side],
+            row_sems,
+            (side,),
+            (s + 2 * side - 1, g),
+        )
+
+    for ds in (-1, 1):
+
+        @pl.when(has(ds))
+        def _():
+            row_copy((ds + 1) // 2).start()
+            for k in range(n_girth):
+                packet_copy(ds, k).start()
+
+    for side in (0, 1):
+        edge_copy(side).start()
+    for k in range(1, n_girth):
+        packet_copy(0, k).start()
 
     def team_copy(out, into, sems, k):
         q = lax.rem(place + k, TEAM)
@@ -280,6 +287,8 @@
         )
         outer.append([jnp.where(has(o - 1), x, 0.0) for x in found])
 
+    for n in (5, 6, 7, 8, 10, 11):
+        load(n).wait()
     for r in range(ROWS):
         here = cells[r]
         before = outer[0] if r == 0 else cells[r - 1]
@@ -318,6 +327,11 @@
     for k in range(1, TEAM):
         team_copy(rhs_out, rhs_in, rhs_sems, k).start()
     own_copy(rhs_out, rhs_in, 1).start()
+    keep = [
+        pltpu.make_async_copy(new_state, results[0], store_sems.at[0]),
+        pltpu.make_async_copy(residual_out, results[1], store_sems.at[1]),
+    ]
+    keep[1].start()
 
     for k in range(1, TEAM):
         team_copy(inv_out, inv_in, inv_sems, TEAM - k).wait_send()
@@ -446,6 +460,8 @@
             at = (r * VARS + v) * 8
             new_state[at : at + 8, :] = current[at : at + 8, :] + upd_in[r, pl.ds(v, 8, stride=8), :]
 
+    keep[0].start()
+
     for k in range(1, TEAM):
         upd_copy(k).wait_send()
     for side in (0, 1):
@@ -465,6 +481,20 @@
         @pl.when(there)
         def _():
             link_copy(way).wait_send()
+
+    for copy in keep:
+        copy.wait()
+
+
+def store(a, b, a_out, b_out, sems):
+    copies = [
+        pltpu.make_async_copy(a, a_out, sems.at[0]),
+        pltpu.make_async_copy(b, b_out, sems.at[1]),
+    ]
+    for copy in copies:
+        copy.start()
+    for copy in copies:
+        copy.wait()
 
 
 def per_device(
@@ -483,17 +513,38 @@
 ):
     n_stream, n_girth = lax.axis_size("stream"), lax.axis_size("girth")
     f32 = jnp.float32
-    vmem = pl.BlockSpec(memory_space=pltpu.VMEM)
-    smem = pl.BlockSpec(memory_space=pltpu.SMEM)
+    hbm = pl.BlockSpec(memory_space=pltpu.HBM)
     blocks = ROWS * VARS * 8
     padded = -(-ROWS * VARS * VARS // 8) * 8
     dma = pltpu.SemaphoreType.DMA
+    given = (
+        state.reshape(blocks, 128),
+        propeller,
+        donor_index,
+        fringe_index,
+        donor_weight,
+        disk_mask.reshape(ROWS * 8, 128),
+        thrust,
+        face.reshape(ROWS * 6 * 8, 128),
+        coupling,
+        diag_inverse,
+        lower_jacobian,
+        upper_jacobian,
+    )
+    scalars = (6, 8, 10, 11)
+    held = [
+        (pltpu.SMEM if n in scalars else pltpu.VMEM)(x.shape, x.dtype) for n, x in enumerate(given)
+    ]
+    results = [jax.ShapeDtypeStruct((blocks, 128), f32)] * 2
     new_state, residual = pl.pallas_call(
         functools.partial(kernel, n_stream, n_girth),
-        out_shape=[jax.ShapeDtypeStruct((blocks, 128), f32)] * 2,
-        in_specs=[vmem] * 6 + [smem, vmem, smem, vmem, smem, smem],
-        out_specs=[vmem, vmem],
-        scratch_shapes=[
+        out_shape=results,
+        in_specs=[hbm] * 12,
+        out_specs=[hbm, hbm],
+        scratch_shapes=held
+        + [
+            pltpu.VMEM((blocks, 128), f32),
+            pltpu.VMEM((blocks, 128), f32),
             pltpu.VMEM((8, 128), f32),
             pltpu.VMEM((3, n_girth, 8, 128), f32),
             pltpu.VMEM((2, ROWS, 8, 128), f32),
@@ -520,25 +571,22 @@
             dma((2, TEAM)),
             dma((2, 2)),
             dma((3,)),
+            dma((12,)),
+            dma((2,)),
         ],
         compiler_params=pltpu.CompilerParams(
-            collective_id=0, has_side_effects=True, vmem_limit_bytes=24 * 1024 * 1024
+            collective_id=0, has_side_effects=True, vmem_limit_bytes=60 * 1024 * 1024
         ),
         cost_estimate=pl.CostEstimate(flops=12_000_000, bytes_accessed=500_000, transcendentals=0),
-    )(
-        state.reshape(blocks, 128),
-        propeller,
-        donor_index,
-        fringe_index,
-        donor_weight,
-        disk_mask.reshape(ROWS * 8, 128),
-        thrust,
-        face.reshape(ROWS * 6 * 8, 128),
-        coupling,
-        diag_inverse,
-        lower_jacobian,
-        upper_jacobian,
-    )
+    )(*given)
+    new_state, residual = pl.pallas_call(
+        store,
+        out_shape=results,
+        in_specs=[hbm, hbm],
+        out_specs=[hbm, hbm],
+        scratch_shapes=[dma((2,))],
+        compiler_params=pltpu.CompilerParams(vmem_limit_bytes=60 * 1024 * 1024),
+    )(new_state, residual)
     return new_state.reshape(state.shape), residual.reshape(state.shape)
 
 

time: 32.5 us -> 28.7 us (0.88)
  local copies, waits for them, and re-layouts: 7.93 us -> 0 us
  Pallas kernels: 23.4 us -> 27.9 us
    unnamed x26 -> x0, local copies, waits for them, and re-layouts: 7.93 us -> none
    pallas_call x1 -> x2, Pallas kernels: 23.4 us -> 27.9 us  [the longest x1 23.3 us: per_device(): pl.pallas_call(functools.partial(kernel, n_stream, n_girth), out_shape=re...]
where the time goes in v2:
time: 28.7 us; the launch traced here: 28.5 us
  Pallas kernels  27.9 us (97%)
  between operations  0.64 us (2%)
    pallas_call x1, Pallas kernels, per_device(): pl.pallas_call(functools.partial(kernel, n_stream, n_girth), out_shape=re...  23.3 us
    pallas_call x1, Pallas kernels, per_device(): pl.pallas_call(store, out_shape=results, in_specs=[hbm, hbm], out_specs=[...  4.6 us

profile of v2, /device:TPU:0, one launch (start us, length us, event | category | flops | bytes accessed | tf_op | source)
XLA Modules:
  0.0 28.5 jit_solution(5683087602718904514)
XLA Ops:
  0.6 23.3 %shard_map.131 = (f32[112,128]{1,0:T(8,128)}, f32[112,128]{1,0:T(8,128)}) custom-call(f32[112,128]{1,0:T(8,128)} %bitcast.5, f32[7,256]{1,0:T(8,128)} %refs_1_.1, s32[1,32]{1,0:T(1,128)} %refs_2_.1, s32[1,32]{1,0:T(1,128)} %refs_3_.1, f32[1,32]{1,0:T(1,128)} %refs_4_.1, s32[16,128]{1,0:T(8,128)} %bitcast.7, f32[7]{0:T(128)} %refs_6_.1, f32[96,128]{1,0:T(8,128)} %bitcast.6, ...), custom_call_target="tpu_custom_call" | custom-call | flops 12000000 | bytes 500000 | tf_op jit(solution)/shard_map/pallas_call | solution.py:539
  23.9 4.6 %shard_map.132 = (f32[112,128]{1,0:T(8,128)}, f32[112,128]{1,0:T(8,128)}) custom-call(f32[112,128]{1,0:T(8,128)} %get-tuple-element.6.a, f32[112,128]{1,0:T(8,128)} %get-tuple-element.7.b), custom_call_target="tpu_custom_call" | custom-call | tf_op jit(solution)/shard_map/pallas_call | solution.py:582

commit v3 on v2

--- a/solution.py
+++ b/solution.py
@@ -31,6 +31,7 @@
         packets,
         edge_out,
         edge_in,
+        row_out,
         row_in,
         planes,
         inv_out,
@@ -134,13 +135,17 @@
     taken = jnp.dot(prop[...], chosen, precision=PRECISE, preferred_element_type=jnp.float32)
     packet[0:VARS, :] = taken * jnp.where(live, spread(weight), 0.0)
     packet[VARS : VARS + 1, :] = jnp.where(live, spread(landing) + 1, 0).astype(jnp.float32)
-    packets[1, 0] = packet[...]
 
     load(0).wait()
     for side, at in ((0, 0), (1, 7)):
         for r in range(ROWS):
             edge_out[side, r, 0:VARS, :] = state[pl.ds(r * VARS * 8 + at, VARS, stride=8), :]
             edge_out[side, r, VARS : VARS + 1, :] = jnp.zeros((1, 128), jnp.float32)
+        edge_out[side, ROWS] = packet[...]
+        row_out[side, 0 : VARS * 8, :] = state[
+            side * (ROWS - 1) * VARS * 8 : (side * (ROWS - 1) + 1) * VARS * 8, :
+        ]
+        row_out[side, VARS * 8 :, :] = packet[...]
 
     load(9).wait()
     for r in range(ROWS):
@@ -171,9 +176,8 @@
         )
 
     def row_copy(side):
-        rows = VARS * 8
         return remote(
-            state.at[pl.ds(side * rows, rows)],
+            row_out.at[side],
             row_in.at[side],
             row_sems,
             (side,),
@@ -185,35 +189,47 @@
         @pl.when(has(ds))
         def _():
             row_copy((ds + 1) // 2).start()
-            for k in range(n_girth):
+            for k in range(1, n_girth):
                 packet_copy(ds, k).start()
 
     for side in (0, 1):
         edge_copy(side).start()
-    for k in range(1, n_girth):
+    for k in range(2, n_girth - 1):
         packet_copy(0, k).start()
 
     def team_copy(out, into, sems, k):
         q = lax.rem(place + k, TEAM)
         return remote(out.at[q], into.at[place], sems, (k,), (base + q, g))
 
+    def team_arrival(out, into, sems, k):
+        return pltpu.make_async_remote_copy(
+            src_ref=out.at[place],
+            dst_ref=into.at[lax.rem(place + TEAM - k, TEAM)],
+            send_sem=sems.at[0, k],
+            recv_sem=sems.at[1, k],
+            device_id=(base + lax.rem(place + k, TEAM), g),
+            device_id_type=MESH,
+        )
+
+    far_first = sorted(range(1, TEAM), key=lambda k: -min(k, TEAM - k))
+
     def own_copy(out, into, n):
         return pltpu.make_async_copy(out.at[place], into.at[place], local_sems.at[n])
 
-    for k in range(1, TEAM):
+    for k in far_first:
         team_copy(inv_out, inv_in, inv_sems, k).start()
     own_copy(inv_out, inv_in, 0).start()
 
     for side in (0, 1):
         edge_copy(side).wait_recv()
-    for k in range(1, n_girth):
+    for k in range(2, n_girth - 1):
         packet_copy(0, k).wait_recv()
     for ds in (-1, 1):
 
         @pl.when(has(ds))
         def _():
             row_copy((1 - ds) // 2).wait_recv()
-            for k in range(n_girth):
+            for k in range(1, n_girth):
                 packet_copy(-ds, k).wait_recv()
 
     girth_cell = lax.broadcasted_iota(jnp.int32, (8, 128), 0)
@@ -222,12 +238,19 @@
     var_row = lax.broadcasted_iota(jnp.int32, (8, 128), 0)
     peer = lax.rem(lane, slots) // CAP
 
+    def packet_from(o, k):
+        if o != 1 and k == 0:
+            return row_in[1 - o // 2, VARS * 8 :, :]
+        if o == 1 and k in (1, n_girth - 1):
+            return edge_in[1 if k == 1 else 0, ROWS]
+        return packet[...] if k == 0 else packets[o, k]
+
     def landed(o, plan):
         total = None
         for first in range(0, n_girth, packs):
-            tile = packets[o, first]
+            tile = packet_from(o, first)
             for k in range(first + 1, first + packs):
-                tile = tile + packets[o, k]
+                tile = tile + packet_from(o, k)
             code = tile[VARS : VARS + 1, :].astype(jnp.int32) - 1
             row, gc, nc = code >> 10, (code >> 7) & 7, code & 127
             nc = jnp.where(code >= 0, nc, -1)
@@ -324,7 +347,7 @@
         for c in range(8):
             rhs_out[c // PAIR, r, c % PAIR, 0:VARS, :] = rhs_planes[r, pl.ds(c, VARS, stride=8), :]
 
-    for k in range(1, TEAM):
+    for k in far_first:
         team_copy(rhs_out, rhs_in, rhs_sems, k).start()
     own_copy(rhs_out, rhs_in, 1).start()
     keep = [
@@ -333,22 +356,10 @@
     ]
     keep[1].start()
 
-    for k in range(1, TEAM):
-        team_copy(inv_out, inv_in, inv_sems, TEAM - k).wait_send()
-        pltpu.make_async_remote_copy(
-            src_ref=inv_out.at[place],
-            dst_ref=inv_in.at[lax.rem(place + TEAM - k, TEAM)],
-            send_sem=inv_sems.at[0, k],
-            recv_sem=inv_sems.at[1, k],
-            device_id=(base + lax.rem(place + k, TEAM), g),
-            device_id_type=MESH,
-        ).wait_recv()
-    own_copy(inv_out, inv_in, 0).wait()
-
     def column(k, h, r, j):
         return inv_in[k, h, pl.ds(r * VARS * VARS + j, VARS, stride=VARS), :]
 
-    def matrices(k, carry):
+    def matrices(k):
         for r in range(ROWS):
             for h in range(PAIR):
                 cols = [column(k, h, r, j) for j in range(VARS)]
@@ -359,20 +370,28 @@
                         b = b + cols[j] * upper[j, m]
                     fmap[k, r, h, m, 0:VARS, :] = f
                     bmap[k, r, h, m, 0:VARS, :] = b
+
+    def arrived(step):
+        @pl.when(step == 0)
+        def _():
+            own_copy(inv_out, inv_in, 0).wait()
+
+        for n, k in enumerate(reversed(far_first)):
+
+            @pl.when(step == n + 1)
+            def _():
+                team_arrival(inv_out, inv_in, inv_sems, k).wait()
+
+    def take_blocks(step, carry):
+        arrived(step)
+        away = (step + 1) // 2 * (2 * lax.rem(step + 1, 2) - 1)
+        matrices(lax.rem(place - away + TEAM, TEAM))
         return carry
 
-    lax.fori_loop(0, TEAM, matrices, 0)
+    lax.fori_loop(0, TEAM, take_blocks, 0)
 
     for k in range(1, TEAM):
-        team_copy(rhs_out, rhs_in, rhs_sems, TEAM - k).wait_send()
-        pltpu.make_async_remote_copy(
-            src_ref=rhs_out.at[place],
-            dst_ref=rhs_in.at[lax.rem(place + TEAM - k, TEAM)],
-            send_sem=rhs_sems.at[0, k],
-            recv_sem=rhs_sems.at[1, k],
-            device_id=(base + lax.rem(place + k, TEAM), g),
-            device_id_type=MESH,
-        ).wait_recv()
+        team_arrival(rhs_out, rhs_in, rhs_sems, k).wait()
     own_copy(rhs_out, rhs_in, 1).wait()
 
     def product(matrix, x):
@@ -436,7 +455,7 @@
                 x[h] = stars[k, r, h] + product(lambda m: bmap[k, r, h, m, 0:VARS, :], x[h])
                 upd_out[k, r, h * 8 : h * 8 + VARS, :] = x[h]
     depart(1, team > 0, x)
-    for k in range(1, TEAM):
+    for k in far_first:
         upd_copy(k).start()
     own = pltpu.make_async_copy(
         upd_out.at[place],
@@ -466,14 +485,14 @@
         upd_copy(k).wait_send()
     for side in (0, 1):
         edge_copy(side).wait_send()
-    for k in range(1, n_girth):
+    for k in range(2, n_girth - 1):
         packet_copy(0, k).wait_send()
     for ds in (-1, 1):
 
         @pl.when(has(ds))
         def _():
             row_copy((ds + 1) // 2).wait_send()
-            for k in range(n_girth):
+            for k in range(1, n_girth):
                 packet_copy(ds, k).wait_send()
 
     for way, there in ((0, team < n_teams - 1), (1, team > 0)):
@@ -486,15 +505,18 @@
         copy.wait()
 
 
-def store(a, b, a_out, b_out, sems):
-    copies = [
-        pltpu.make_async_copy(a, a_out, sems.at[0]),
-        pltpu.make_async_copy(b, b_out, sems.at[1]),
+def store(a, b, a_out, b_out, a_held, b_held, sems):
+    steps = [
+        pltpu.make_async_copy(*ends, sems.at[n])
+        for n, ends in enumerate(((a, a_held), (b, b_held), (a_held, a_out), (b_held, b_out)))
     ]
-    for copy in copies:
-        copy.start()
-    for copy in copies:
-        copy.wait()
+    steps[0].start()
+    steps[1].start()
+    for n in range(2):
+        steps[n].wait()
+        steps[n + 2].start()
+    for n in range(2):
+        steps[n + 2].wait()
 
 
 def per_device(
@@ -547,9 +569,10 @@
             pltpu.VMEM((blocks, 128), f32),
             pltpu.VMEM((8, 128), f32),
             pltpu.VMEM((3, n_girth, 8, 128), f32),
-            pltpu.VMEM((2, ROWS, 8, 128), f32),
-            pltpu.VMEM((2, ROWS, 8, 128), f32),
-            pltpu.VMEM((2, VARS * 8, 128), f32),
+            pltpu.VMEM((2, ROWS + 1, 8, 128), f32),
+            pltpu.VMEM((2, ROWS + 1, 8, 128), f32),
+            pltpu.VMEM((2, VARS * 8 + 8, 128), f32),
+            pltpu.VMEM((2, VARS * 8 + 8, 128), f32),
             pltpu.VMEM((padded * 8, 128), f32),
             pltpu.VMEM((TEAM, PAIR, padded, 128), f32),
             pltpu.VMEM((TEAM, PAIR, padded, 128), f32),
@@ -584,7 +607,7 @@
         out_shape=results,
         in_specs=[hbm, hbm],
         out_specs=[hbm, hbm],
-        scratch_shapes=[dma((2,))],
+        scratch_shapes=[pltpu.VMEM((blocks, 128), f32)] * 2 + [dma((4,))],
         compiler_params=pltpu.CompilerParams(vmem_limit_bytes=60 * 1024 * 1024),
     )(new_state, residual)
     return new_state.reshape(state.shape), residual.reshape(state.shape)

time: 28.7 us -> 25.8 us (0.90)
  Pallas kernels: 27.9 us -> 25 us
    pallas_call x1, Pallas kernels: 4.6 us -> 1.5 us  [per_device(): pl.pallas_call(store, out_shape=results, in_specs=[hbm, hbm], out_specs=[...]
where the time goes in v3:
time: 25.8 us; the launch traced here: 25.6 us
  Pallas kernels  25 us (97%)
  between operations  0.64 us (2%)
    pallas_call x1, Pallas kernels, per_device(): pl.pallas_call(functools.partial(kernel, n_stream, n_girth), out_shape=re...  23.5 us
    pallas_call x1, Pallas kernels, per_device(): pl.pallas_call(store, out_shape=results, in_specs=[hbm, hbm], out_specs=[...  1.5 us

profile of v3, /device:TPU:0, one launch (start us, length us, event | category | flops | bytes accessed | tf_op | source)
XLA Modules:
  0.0 25.6 jit_solution(10879755832137631253)
XLA Ops:
  0.6 23.5 %shard_map.131 = (f32[112,128]{1,0:T(8,128)}, f32[112,128]{1,0:T(8,128)}) custom-call(f32[112,128]{1,0:T(8,128)} %bitcast.5, f32[7,256]{1,0:T(8,128)} %refs_1_.1, s32[1,32]{1,0:T(1,128)} %refs_2_.1, s32[1,32]{1,0:T(1,128)} %refs_3_.1, f32[1,32]{1,0:T(1,128)} %refs_4_.1, s32[16,128]{1,0:T(8,128)} %bitcast.7, f32[7]{0:T(128)} %refs_6_.1, f32[96,128]{1,0:T(8,128)} %bitcast.6, ...), custom_call_target="tpu_custom_call" | custom-call | flops 12000000 | bytes 500000 | tf_op jit(solution)/shard_map/pallas_call | solution.py:561
  24.1 1.5 %shard_map.132 = (f32[112,128]{1,0:T(8,128)}, f32[112,128]{1,0:T(8,128)}) custom-call(f32[112,128]{1,0:T(8,128)} %get-tuple-element.6.a, f32[112,128]{1,0:T(8,128)} %get-tuple-element.7.b), custom_call_target="tpu_custom_call" | custom-call | tf_op jit(solution)/shard_map/pallas_call | solution.py:605

commit v4 on v3

--- a/solution.py
+++ b/solution.py
@@ -11,8 +11,8 @@
 PRECISE = lax.Precision.HIGHEST
 VARS = 7
 ROWS = 2
-TEAM = 4
-PAIR = 2
+TEAM = 8
+PAIR = 1
 CAP = 8
 
 
@@ -503,20 +503,6 @@
 
     for copy in keep:
         copy.wait()
-
-
-def store(a, b, a_out, b_out, a_held, b_held, sems):
-    steps = [
-        pltpu.make_async_copy(*ends, sems.at[n])
-        for n, ends in enumerate(((a, a_held), (b, b_held), (a_held, a_out), (b_held, b_out)))
-    ]
-    steps[0].start()
-    steps[1].start()
-    for n in range(2):
-        steps[n].wait()
-        steps[n + 2].start()
-    for n in range(2):
-        steps[n + 2].wait()
 
 
 def per_device(
@@ -602,14 +588,6 @@
         ),
         cost_estimate=pl.CostEstimate(flops=12_000_000, bytes_accessed=500_000, transcendentals=0),
     )(*given)
-    new_state, residual = pl.pallas_call(
-        store,
-        out_shape=results,
-        in_specs=[hbm, hbm],
-        out_specs=[hbm, hbm],
-        scratch_shapes=[pltpu.VMEM((blocks, 128), f32)] * 2 + [dma((4,))],
-        compiler_params=pltpu.CompilerParams(vmem_limit_bytes=60 * 1024 * 1024),
-    )(new_state, residual)
     return new_state.reshape(state.shape), residual.reshape(state.shape)
 
 

time: 25.8 us -> 27.2 us (1.054)
  local copies, waits for them, and re-layouts: 0 us -> 2.09 us
  Pallas kernels: 25 us -> 24.3 us
    unnamed x0 -> x4, local copies, waits for them, and re-layouts: none -> 2.09 us
    pallas_call x1 -> x0, Pallas kernels: 1.5 us -> none  [per_device(): pl.pallas_call(store, out_shape=results, in_specs=[hbm, hbm], out_specs=[...]
    pallas_call x1, Pallas kernels: 23.5 us -> 24.3 us  [per_device(): pl.pallas_call(functools.partial(kernel, n_stream, n_girth), out_shape=re...]
where the time goes in v4:
time: 27.2 us; the launch traced here: 27 us
  Pallas kernels  24.3 us (89%)
  local copies, waits for them, and re-layouts  2.09 us (8%)
  between operations  0.65 us (2%)
    pallas_call x1, Pallas kernels, per_device(): pl.pallas_call(functools.partial(kernel, n_stream, n_girth), out_shape=re...  24.3 us
    unnamed x4, local copies, waits for them, and re-layouts  2.09 us

profile of v4, /device:TPU:0, one launch (start us, length us, event | category | flops | bytes accessed | tf_op | source)
XLA Modules:
  0.0 27.0 jit_solution(1575112280136362363)
XLA Ops:
  0.6 24.3 %shard_map.131 = (f32[112,128]{1,0:T(8,128)}, f32[112,128]{1,0:T(8,128)}) custom-call(f32[112,128]{1,0:T(8,128)} %bitcast.7, f32[7,256]{1,0:T(8,128)} %refs_1_.1, s32[1,32]{1,0:T(1,128)} %refs_2_.1, s32[1,32]{1,0:T(1,128)} %refs_3_.1, f32[1,32]{1,0:T(1,128)} %refs_4_.1, s32[16,128]{1,0:T(8,128)} %bitcast.9, f32[7]{0:T(128)} %refs_6_.1, f32[96,128]{1,0:T(8,128)} %bitcast.8, ...), custom_call_target="tpu_custom_call" | custom-call | flops 12000000 | bytes 500000 | tf_op jit(solution)/shard_map/pallas_call | solution.py:547
  24.9 0.0 copy-start
  24.9 1.5 %copy.16 = f32[2,7,8,128]{3,2,1,0:T(8,128)} copy(f32[2,7,8,128]{3,2,1,0:T(8,128)} %bitcast.6) | data formatting | bytes 114688
  26.4 0.0 copy-done
  26.4 0.6 %copy.17 = f32[2,7,8,128]{3,2,1,0:T(8,128)} copy(f32[2,7,8,128]{3,2,1,0:T(8,128)S(1)} %bitcast.5) | data formatting | bytes 114688
Async XLA Ops:
  24.9 1.5 %copy-start = (f32[112,128]{1,0:T(8,128)S(1)}, f32[112,128]{1,0:T(8,128)}, u32[]{:S(2)}) copy-start(f32[112,128]{1,0:T(8,128)} %get-tuple-element.5) | copy-start | bytes 172036

commit v5 on v3

--- a/solution.py
+++ b/solution.py
@@ -42,6 +42,8 @@
         rhs_in,
         fmap,
         bmap,
+        reply,
+        answer,
         upd_out,
         upd_in,
         link_out,
@@ -438,23 +440,73 @@
             (base + q, g),
         )
 
-    x = arrive(0, team > 0)
-    stars = {}
-    for k in range(TEAM):
-        for r in range(ROWS):
+    last = team == n_teams - 1
+    steps = TEAM * ROWS
+    row_of = lax.broadcasted_iota(jnp.int32, (VARS, 128), 0)
+    unit = tuple(jnp.where(row_of == n, 1.0, 0.0) for _ in range(PAIR) for n in range(VARS))
+
+    def factor(maps, t, h):
+        return lambda m: maps[t // ROWS, lax.rem(t, ROWS), h, m, 0:VARS, :]
+
+    def forward(x):
+        stars = []
+        for t in range(steps):
+            k, r = divmod(t, ROWS)
+            x = [offsets[k, r, h] + product(factor(fmap, t, h), x[h]) for h in range(PAIR)]
+            stars.append(x)
+        return stars
+
+    def backward(stars):
+        x, updates = stars[-1], [stars[-1]]
+        for t in reversed(range(steps - 1)):
+            x = [stars[t][h] + product(factor(bmap, t, h), x[h]) for h in range(PAIR)]
+            updates.append(x)
+        return updates[::-1]
+
+    def respond(maps, into, start, reverse, plus=None):
+        def advance(n, columns):
+            t = steps - 1 - n if reverse else n
+            out = []
             for h in range(PAIR):
-                x[h] = offsets[k, r, h] + product(
-                    lambda m: fmap[k, r, h, m, 0:VARS, :], x[h]
-                )
-                stars[k, r, h] = x[h]
-    depart(0, team < n_teams - 1, x)
-    x = arrive(1, team < n_teams - 1)
-    for k in reversed(range(TEAM)):
-        for r in reversed(range(ROWS)):
+                for v in range(VARS):
+                    x = product(factor(maps, t, h), columns[h * VARS + v])
+                    if plus is not None:
+                        x = x + factor(plus, t, h)(v)
+                    into[t // ROWS, lax.rem(t, ROWS), h, v, 0:VARS, :] = x
+                    out.append(x)
+            return tuple(out)
+
+        lax.fori_loop(0, steps, advance, start)
+
+    def finish(updates, entering):
+        first = None
+        for t in range(steps):
+            k, r = divmod(t, ROWS)
+            x = [
+                updates[t][h] + product(factor(answer, t, h), entering[h]) for h in range(PAIR)
+            ]
             for h in range(PAIR):
-                x[h] = stars[k, r, h] + product(lambda m: bmap[k, r, h, m, 0:VARS, :], x[h])
                 upd_out[k, r, h * 8 : h * 8 + VARS, :] = x[h]
-    depart(1, team > 0, x)
+            if t == 0:
+                depart(1, team > 0, x)
+
+    nothing = [jnp.zeros((VARS, 128), jnp.float32)] * PAIR
+
+    @pl.when(last)
+    def _():
+        updates = backward(forward(nothing))
+        respond(fmap, reply, unit, False)
+        respond(bmap, answer, tuple(jnp.zeros_like(x) for x in unit), True, reply)
+        finish(updates, arrive(0, team > 0))
+
+    @pl.when(jnp.logical_not(last))
+    def _():
+        stars = forward(arrive(0, team > 0))
+        depart(0, team < n_teams - 1, stars[-1])
+        updates = backward(stars)
+        respond(bmap, answer, unit, True)
+        finish(updates, arrive(1, team < n_teams - 1))
+
     for k in far_first:
         upd_copy(k).start()
     own = pltpu.make_async_copy(
@@ -582,6 +634,8 @@
             pltpu.VMEM((TEAM, ROWS, PAIR, 8, 128), f32),
             pltpu.VMEM((TEAM, ROWS, PAIR, VARS, 8, 128), f32),
             pltpu.VMEM((TEAM, ROWS, PAIR, VARS, 8, 128), f32),
+            pltpu.VMEM((TEAM, ROWS, PAIR, VARS, 8, 128), f32),
+            pltpu.VMEM((TEAM, ROWS, PAIR, VARS, 8, 128), f32),
             pltpu.VMEM((TEAM, ROWS, PAIR * 8, 128), f32),
             pltpu.VMEM((ROWS, TEAM * PAIR * 8, 128), f32),
             pltpu.VMEM((2, PAIR, 8, 128), f32),

time: 25.8 us -> 25.7 us (level)
  no operation moved by 1% of the time
where the time goes in v5:
time: 25.7 us; the launch traced here: 25.5 us
  Pallas kernels  24.8 us (96%)
  between operations  0.64 us (2%)
    pallas_call x1, Pallas kernels, per_device(): pl.pallas_call(functools.partial(kernel, n_stream, n_girth), out_shape=re...  23.3 us
    pallas_call x1, Pallas kernels, per_device(): pl.pallas_call(store, out_shape=results, in_specs=[hbm, hbm], out_specs=[...  1.5 us

profile of v5, /device:TPU:0, one launch (start us, length us, event | category | flops | bytes accessed | tf_op | source)
XLA Modules:
  0.0 25.5 jit_solution(7931061507700540689)
XLA Ops:
  0.6 23.3 %shard_map.131 = (f32[112,128]{1,0:T(8,128)}, f32[112,128]{1,0:T(8,128)}) custom-call(f32[112,128]{1,0:T(8,128)} %bitcast.5, f32[7,256]{1,0:T(8,128)} %refs_1_.1, s32[1,32]{1,0:T(1,128)} %refs_2_.1, s32[1,32]{1,0:T(1,128)} %refs_3_.1, f32[1,32]{1,0:T(1,128)} %refs_4_.1, s32[16,128]{1,0:T(8,128)} %bitcast.7, f32[7]{0:T(128)} %refs_6_.1, f32[96,128]{1,0:T(8,128)} %bitcast.6, ...), custom_call_target="tpu_custom_call" | custom-call | flops 12000000 | bytes 500000 | tf_op jit(solution)/shard_map/pallas_call | solution.py:613
  24.0 1.5 %shard_map.132 = (f32[112,128]{1,0:T(8,128)}, f32[112,128]{1,0:T(8,128)}) custom-call(f32[112,128]{1,0:T(8,128)} %get-tuple-element.6.a, f32[112,128]{1,0:T(8,128)} %get-tuple-element.7.b), custom_call_target="tpu_custom_call" | custom-call | tf_op jit(solution)/shard_map/pallas_call | solution.py:659

commit v6 on v3

--- a/solution.py
+++ b/solution.py
@@ -224,14 +224,6 @@
         edge_copy(side).wait_recv()
     for k in range(2, n_girth - 1):
         packet_copy(0, k).wait_recv()
-    for ds in (-1, 1):
-
-        @pl.when(has(ds))
-        def _():
-            row_copy((1 - ds) // 2).wait_recv()
-            for k in range(1, n_girth):
-                packet_copy(-ds, k).wait_recv()
-
     girth_cell = lax.broadcasted_iota(jnp.int32, (8, 128), 0)
     normal_cell = lax.broadcasted_iota(jnp.int32, (8, 128), 1)
     normal_rows = lax.broadcasted_iota(jnp.int32, (128, 128), 0)
@@ -303,6 +295,14 @@
             beside[side, r] = jnp.where(
                 found[VARS : VARS + 1] > 0.5, found, edge_in[1 - side, r]
             )
+    for ds in (-1, 1):
+
+        @pl.when(has(ds))
+        def _():
+            row_copy((1 - ds) // 2).wait_recv()
+            for k in range(1, n_girth):
+                packet_copy(-ds, k).wait_recv()
+
     outer = []
     for o, r, side in ((0, 1, 1), (2, 0, 0)):
         found, _ = settle(

time: 25.8 us -> 25.7 us (level)
  no operation moved by 1% of the time
where the time goes in v6:
time: 25.7 us; the launch traced here: 25.5 us
  Pallas kernels  24.9 us (97%)
  between operations  0.64 us (2%)
    pallas_call x1, Pallas kernels, per_device(): pl.pallas_call(functools.partial(kernel, n_stream, n_girth), out_shape=re...  23.4 us
    pallas_call x1, Pallas kernels, per_device(): pl.pallas_call(store, out_shape=results, in_specs=[hbm, hbm], out_specs=[...  1.5 us

profile of v6, /device:TPU:0, one launch (start us, length us, event | category | flops | bytes accessed | tf_op | source)
XLA Modules:
  0.0 25.5 jit_solution(1432776431674546187)
XLA Ops:
  0.6 23.4 %shard_map.131 = (f32[112,128]{1,0:T(8,128)}, f32[112,128]{1,0:T(8,128)}) custom-call(f32[112,128]{1,0:T(8,128)} %bitcast.5, f32[7,256]{1,0:T(8,128)} %refs_1_.1, s32[1,32]{1,0:T(1,128)} %refs_2_.1, s32[1,32]{1,0:T(1,128)} %refs_3_.1, f32[1,32]{1,0:T(1,128)} %refs_4_.1, s32[16,128]{1,0:T(8,128)} %bitcast.7, f32[7]{0:T(128)} %refs_6_.1, f32[96,128]{1,0:T(8,128)} %bitcast.6, ...), custom_call_target="tpu_custom_call" | custom-call | flops 12000000 | bytes 500000 | tf_op jit(solution)/shard_map/pallas_call | solution.py:561
  24.0 1.5 %shard_map.132 = (f32[112,128]{1,0:T(8,128)}, f32[112,128]{1,0:T(8,128)}) custom-call(f32[112,128]{1,0:T(8,128)} %get-tuple-element.6.a, f32[112,128]{1,0:T(8,128)} %get-tuple-element.7.b), custom_call_target="tpu_custom_call" | custom-call | tf_op jit(solution)/shard_map/pallas_call | solution.py:605
